TPU v7x, 512 devices: a whole 4x4x16 slice. The times are simulated.
512 devices in a mesh: section: 8 (over z_lo), mp: 64 (over x, z_hi, y, core).
Axes of the slice: x: 4, y: 4, z: 16 (z_hi: 2, z_lo: 8; z = z_hi * 8 + z_lo), core: 2. Of those that a mesh axis runs over, the one named last changes fastest.
Arguments:
- latents: float32 [8, 64, 64, 96], P('section', 'mp'), may hold values from -6 to 6
- renoise: float32 [8, 64, 64, 96], P('section', 'mp'), may hold values from -6 to 6
- finished: float32 [64, 64, 96], P('mp', None, 'section'), may hold values from -6 to 6
- cache_keys: bfloat16 [64, 192, 768], P('mp'), may hold values from -160 to 160
- cache_values: bfloat16 [64, 192, 768], P('mp'), may hold values from -5 to 5
- window_start: int32 [64], P('mp'), may hold values from 0 to 5
- window_count: int32 [64], P('mp'), may hold values from 0 to 6, as said below
- timesteps: int32 [8], replicated, may hold values from 1 to 999, as said below
- w_in: bfloat16 [64, 1536], replicated, may hold values from -0.75 to 0.75
- w_time: bfloat16 [256, 7680], P(None, 'mp'), may hold values from -0.375 to 0.375
- w_qkv: bfloat16 [1536, 2304], P(('section', 'mp')), may hold values from -0.15625 to 0.15625
- wo_rows: bfloat16 [1536, 768], P('mp'), may hold values from -0.21875 to 0.21875
- w_out: bfloat16 [1536, 64], replicated, may hold values from -0.15625 to 0.15625
Outputs:
- next_latents: float32 [8, 64, 64, 96], P('section', 'mp')
Inputs may be any that keep to these rules, and one draw needn't show every extreme that they name: `timesteps`: strictly decreasing along the steps; the first step's is 900 or more. `window_count`: some stream has all 6 frames valid and some stream none.
All inputs are finite; a program needn't handle non-finite values.
Results may differ from a plain program's by a relative error of at most 0.0065.
Values may be sent and summed in bfloat16 or wider, within the bound.
No kernel may reach another device: no remote copies, remote signals or barrier semaphores. Data moves between devices by JAX's collectives and lax.ppermute only.
A program may use at most 64 MiB of HBM per device.

v0:
```python
import math

import jax
import jax.numpy as jnp
from jax import lax
from jax.sharding import PartitionSpec as P

HEADS = 6
CACHE_FR = 6
FRAME_TOK = 32


def from_behind(array, axis, by):
    devices = lax.axis_size(axis)
    return lax.ppermute(array, axis, [(i, (i + by) % devices) for i in range(devices)])


def sinusoid(time_values, freq_count):
    half_count = freq_count // 2
    frequency = jnp.exp(-math.log(10000.0) * jnp.arange(half_count, dtype=jnp.float32) / half_count)
    phase_grid = time_values.astype(jnp.float32)[:, None] * frequency[None, :]
    return jnp.concatenate([jnp.cos(phase_grid), jnp.sin(phase_grid)], axis=1)


def layer_norm(values):
    middle = jnp.mean(values, axis=-1, keepdims=True)
    centered = values - middle
    spread = jnp.mean(centered * centered, axis=-1, keepdims=True)
    return centered * lax.rsqrt(spread + 1e-06)


def fold_rows(own_rows, done_rows, inner_width):

    def add_rows(running, segment, offset):
        first_sum = jnp.dot(own_rows, segment, preferred_element_type=jnp.float32)
        second_sum = jnp.dot(
            done_rows, segment[:, inner_width:], preferred_element_type=jnp.float32
        )
        return (first_sum, second_sum)

    return add_rows


def attend(queries, key_rows, value_rows, key_mask, head_count):
    row_count, inner_width = queries.shape
    head_size = inner_width // head_count

    def one_head(head_pos):
        begin = head_pos * head_size
        query_part = lax.dynamic_slice_in_dim(queries, begin, head_size, 1)
        key_part = lax.dynamic_slice_in_dim(key_rows, begin, head_size, 1)
        value_part = lax.dynamic_slice_in_dim(value_rows, begin, head_size, 1)
        scores = lax.dot_general(
            query_part, key_part, (((1,), (1,)), ((), ())), preferred_element_type=jnp.float32
        ) * (1.0 / math.sqrt(head_size))
        scores = jnp.where(key_mask[None, :], scores, -jnp.inf)
        highest = jnp.max(scores, axis=-1, keepdims=True)
        weights = jnp.exp(scores - highest)
        probabilities = (weights / jnp.sum(weights, axis=-1, keepdims=True)).astype(jnp.bfloat16)
        return jnp.dot(probabilities, value_part, preferred_element_type=jnp.float32).astype(
            jnp.bfloat16
        )

    pieces = lax.map(one_head, jnp.arange(head_count))
    return pieces.transpose(1, 0, 2).reshape(row_count, inner_width)


def per_device(
    latents,
    renoise,
    finished,
    cache_keys,
    cache_values,
    window_start,
    window_count,
    timesteps,
    w_in,
    w_time,
    w_qkv,
    wo_rows,
    w_out,
):
    section_count = lax.axis_size("section")
    section_pos = lax.axis_index("section")
    model_width = w_in.shape[1]
    inner_width = wo_rows.shape[1]
    time_now = timesteps[section_pos]
    time_next = jnp.where(
        section_pos + 1 < section_count,
        timesteps[jnp.minimum(section_pos + 1, section_count - 1)],
        0,
    )
    sigma_now = time_now.astype(jnp.float32) / 1000.0
    sigma_next = time_next.astype(jnp.float32) / 1000.0
    time_pair = jnp.stack([time_now, jnp.zeros_like(time_now)])
    local_mod = jnp.dot(
        sinusoid(time_pair, w_time.shape[0]),
        w_time.astype(jnp.float32),
        precision=lax.Precision.HIGHEST,
    )
    modulation = lax.all_gather(local_mod, "mp", axis=1, tiled=True)
    shift_now = modulation[0, :model_width]
    scale_now = modulation[0, model_width : 2 * model_width]
    gate_now = modulation[0, 2 * model_width : 3 * model_width]
    out_shift = modulation[0, 3 * model_width : 4 * model_width]
    out_scale = modulation[0, 4 * model_width : 5 * model_width]
    rest_shift = modulation[1, :model_width]
    rest_scale = modulation[1, model_width : 2 * model_width]
    current = latents[0, 0]
    tokens = current.shape[1]
    hidden = jnp.dot(current.astype(jnp.bfloat16).T, w_in, preferred_element_type=jnp.float32)
    normed = (layer_norm(hidden) * (1.0 + scale_now) + shift_now).astype(jnp.bfloat16)
    source = lax.all_gather(finished[0].astype(jnp.bfloat16), "section", axis=1, tiled=True)
    fresh_hidden = jnp.dot(source.T, w_in, preferred_element_type=jnp.float32)
    fresh_normed = (layer_norm(fresh_hidden) * (1.0 + rest_scale) + rest_shift).astype(jnp.bfloat16)
    initial = (
        jnp.zeros((tokens, 3 * inner_width), jnp.float32),
        jnp.zeros((fresh_normed.shape[0], 2 * inner_width), jnp.float32),
    )
    add_rows = fold_rows(normed, fresh_normed, inner_width)
    own_sum, done_sum = add_rows(
        initial, lax.all_gather(w_qkv, ("section", "mp"), axis=0, tiled=True), jnp.int32(0)
    )
    projected = own_sum.astype(jnp.bfloat16)
    finished_kv = done_sum.astype(jnp.bfloat16)
    frame_index = jnp.arange(cache_keys.shape[1]) // FRAME_TOK
    valid_slots = (frame_index - window_start[0] + CACHE_FR) % CACHE_FR < window_count[0]
    key_mask = jnp.concatenate([valid_slots, jnp.ones((2 * tokens,), dtype=bool)], axis=0)
    key_rows = jnp.concatenate(
        [cache_keys[0], finished_kv[:, :inner_width], projected[:, inner_width : 2 * inner_width]],
        axis=0,
    )
    value_rows = jnp.concatenate(
        [cache_values[0], finished_kv[:, inner_width:], projected[:, 2 * inner_width :]], axis=0
    )
    mixture = attend(projected[:, :inner_width], key_rows, value_rows, key_mask, HEADS)
    attended = lax.dot_general(
        mixture,
        lax.all_gather(wo_rows, "mp", axis=0, tiled=True),
        (((1,), (1,)), ((), ())),
        preferred_element_type=jnp.float32,
    )
    hidden_after = hidden + gate_now * attended
    final_normed = (layer_norm(hidden_after) * (1.0 + out_scale) + out_shift).astype(jnp.bfloat16)
    velocity = lax.dot_general(
        w_out, final_normed, (((0,), (1,)), ((), ())), preferred_element_type=jnp.float32
    )
    stepped = (1.0 - sigma_next) * (current - sigma_now * velocity) + sigma_next * renoise[0, 0]
    handed = from_behind(stepped, "section", 1)
    return handed[None, None]


def solution(mesh):
    in_specs = (
        P("section", "mp", None, None),
        P("section", "mp", None, None),
        P("mp", None, "section"),
        P("mp", None, None),
        P("mp", None, None),
        P("mp"),
        P("mp"),
        P(),
        P(),
        P(None, "mp"),
        P(("section", "mp"), None),
        P("mp", None),
        P(),
    )
    out_specs = P("section", "mp", None, None)
    return jax.shard_map(
        per_device, mesh=mesh, in_specs=in_specs, out_specs=out_specs, check_vma=False
    )
```

profile of v0, /device:TPU:1, one launch (start us, length us, event | category | flops | bytes accessed | tf_op | source)
XLA Modules:
  0.0 979.7 jit_solution(6386953633366617743)
XLA Ops:
  6.5 0.0 copy-start
  6.5 0.0 all-gather.8.cloned.1.call-start
  6.5 0.7 all-gather.8.cloned.1.call-update
  7.3 0.0 all-gather.6.cloned.1.call-start
  7.3 0.7 all-gather.6.cloned.1.call-update
  9.3 1.4 fusion.53
  12.0 0.7 add_convert_fusion.6
  12.7 0.7 convert_element_type.51
  13.4 43.7 %all-gather = bf16[1,64,96]{1,0,2:T(2,128)(2,1)S(1)} all-gather(bf16[1,64,12]{1,0,2:T(2,128)(2,1)S(1)} %convert_element_type.51), channel_id=2, replica_groups=mesh['section'=8,'mp'=64] {'section'}, dimensions={2}, use_global_device_ids=true | all-gather | bytes 13824 | tf_op jit(solution)/shard_map/all_gather | solution.py:113
  57.1 0.1 copy.18
  57.2 0.1 multiply_cosine_fusion
  57.4 1.0 convolution_bitcast_fusion
  58.3 168.3 %all-gather.1 = f32[64,120,2]{1,2,0:T(2,128)S(1)} all-gather(f32[1,120,2]{1,2,0:T(2,128)S(1)} %convolution_bitcast_fusion), channel_id=1, replica_groups=mesh['section'=8,'mp'=64] {'mp'}, dimensions={0}, use_global_device_ids=true | all-gather | bytes 62400 | tf_op jit(solution)/shard_map/all_gather | solution.py:101
  226.6 0.1 reshape.72
  226.8 0.1 fusion.38
  226.9 0.0 copy-done
  226.9 0.3 fusion.55
  227.3 0.2 multiply_reduce_fusion.1
  227.5 1.1 fusion.54
  228.6 0.2 multiply_reduce_fusion.2
  228.9 608.6 %all-gather.8.cloned.1.call-done = bf16[512,3,2304]{2,1,0:T(4,128)(2,1)} async-done(((bf16[1,3,2304]{2,1,0:T(4,128)(2,1)}), bf16[512,3,2304]{2,1,0:T(4,128)(2,1)}) %all-gather.8.cloned.1.call-update) | async-done | bytes 7077904 | tf_op jit(solution)/shard_map/all_gather | solution.py:122
  837.5 17.0 %reshape.74 = bf16[1536,2304]{1,0:T(8,128)(2,1)} reshape(bf16[512,3,2304]{2,1,0:T(4,128)(2,1)} %all-gather.8.cloned.1.call-done) | data formatting | bytes 14155776
  854.5 3.4 fusion.14
  857.9 1.0 copy-done.1
  858.9 1.4 convolution_convert_fusion.1
  860.3 0.0 copy-done.2
  860.3 0.0 copy-done.3
  860.3 0.1 pad_maximum_fusion
  860.4 12.6 %while.10 = (s32[]{:T(128)}, bf16[6,96,128]{2,1,0:T(8,128)(2,1)S(1)}, pred[384]{0:T(512)(128)(4,1)S(1)}, s32[6]{0:T(128)S(1)}, bf16[96,768]{1,0:T(8,128)(2,1)S(1...) while((s32[]{:T(128)}, ...), condition=%wide.region_7.8_spmd, body=%wide.region_4.7_spmd.sunk | while | flops 19181380 | bytes 692023 | solution.py:64
  860.5 0.7 dynamic_slice.40
  861.8 0.3 fusion.73
  862.1 0.2 fusion.74
  862.3 0.2 fusion.75
  862.6 0.7 dynamic_slice.40
  863.9 0.3 fusion.73
  864.2 0.2 fusion.74
  864.4 0.2 fusion.75
  864.7 0.7 dynamic_slice.40
  866.0 0.3 fusion.73
  866.3 0.2 fusion.74
  866.5 0.2 fusion.75
  866.8 0.7 dynamic_slice.40
  868.1 0.3 fusion.73
  868.4 0.2 fusion.74
  868.6 0.2 fusion.75
  868.9 0.7 dynamic_slice.40
  870.2 0.3 fusion.73
  870.5 0.2 fusion.74
  870.7 0.2 fusion.75
  871.0 0.7 dynamic_slice.40
  872.3 0.3 fusion.73
  872.6 0.2 fusion.74
  872.8 0.3 fusion.75
  873.1 0.0 copy-start.4
  873.1 0.0 copy-start.5
  873.1 0.0 copy-start.6
  873.1 84.7 %all-gather.6.cloned.1.call-done = bf16[1536,768]{1,0:T(8,128)(2,1)} async-done(((bf16[24,768]{1,0:T(8,128)(2,1)}), bf16[1536,768]{1,0:T(8,128)(2,1)}) %all-gather.6.cloned.1.call-update) | async-done | bytes 2359312 | tf_op jit(solution)/shard_map/all_gather | solution.py:139
  957.8 2.6 fusion.56
  960.4 0.2 multiply_reduce_fusion
  960.6 0.0 copy-done.4
  960.7 0.3 fusion.20
  961.0 1.9 collective-permute-start
  962.9 9.3 collective-permute-done
  972.3 0.6 copy.37
  (19 shorter events, 0.1 us)
Async XLA Ops:
  6.5 220.4 %copy-start = (bf16[64,1536]{1,0:T(8,128)(2,1)S(1)}, bf16[64,1536]{1,0:T(8,128)(2,1)}, u32[]{:S(2)}) copy-start(bf16[64,1536]{1,0:T(8,128)(2,1)} %param.23) | copy-start | bytes 589828
  6.5 831.0 %all-gather.8.cloned.1.call-start = ((), (), s32[]{:S(2)}) async-start(), calls=%async_computation.1 | async-start | bytes 9455616 | tf_op jit(solution)/shard_map/all_gather | solution.py:122
  7.3 950.5 %all-gather.6.cloned.1.call-start = ((), (), s32[]{:S(2)}) async-start(), calls=%async_computation | async-start | bytes 2396160 | tf_op jit(solution)/shard_map/all_gather | solution.py:139
  854.5 4.4 copy-start.1
  858.9 1.4 copy-start.2
  858.9 1.4 copy-start.3
  873.1 87.6 %copy-start.4 = (bf16[1536,64]{0,1:T(8,128)(2,1)S(1)}, bf16[1536,64]{0,1:T(8,128)(2,1)}, u32[]{:S(2)}) copy-start(bf16[1536,64]{0,1:T(8,128)(2,1)} %param.27) | copy-start | bytes 589828
  873.1 87.6 %copy-start.5 = (f32[1,1,64,96]{3,2,1,0:T(8,128)S(1)}, f32[1,1,64,96]{3,2,1,0:T(8,128)}, u32[]{:S(2)}) copy-start(f32[1,1,64,96]{3,2,1,0:T(8,128)} %param.15) | copy-start | bytes 73732
  873.1 87.6 %copy-start.6 = (f32[1,1,64,96]{3,2,1,0:T(8,128)S(1)}, f32[1,1,64,96]{3,2,1,0:T(8,128)}, u32[]{:S(2)}) copy-start(f32[1,1,64,96]{3,2,1,0:T(8,128)} %param.16) | copy-start | bytes 73732
  961.0 11.3 %collective-permute-start = (f32[64,96]{1,0:T(8,128)S(1)}, f32[64,96]{1,0:T(8,128)S(1)}, u32[]{:S(2)}, u32[]{:S(2)}) collective-permute-start(f32[64,96]{1,0:T(8,128)S(1)} %fusion.20), channel_id=1, source_target_pairs={{0,64},{64,128},{128,192},{192,256},{256,320},{320,384},{384,448},... | collective-permute-start | bytes 73736 | tf_op jit(solution)/shard_map/ppermute | solution.py:15
Sparse Core Ops, SparseCore 0:
  9.6 827.8 all-gather.7
  841.9 115.8 all-gather.5
where the time goes:
time: 981 us; the launch traced here: 980 us
  waiting for transfers between devices  704 us (72%)
  blocking collectives  212 us (22%)
  local copies, waits for them, and re-layouts  24.3 us (2%)
  between operations  16.2 us (2%)
  matrix products  13.3 us (1%)
    all_gather x1, waiting for transfers between devices, per_device(): lax.all_gather(w_qkv, ('section', 'mp'), axis=0, tiled=True)  609 us
    all_gather x1, blocking collectives, per_device(): modulation = lax.all_gather(local_mod, 'mp', axis=1, tiled=True)  168 us
    all_gather x1, waiting for transfers between devices, per_device(): lax.all_gather(wo_rows, 'mp', axis=0, tiled=True)  84.7 us
    all_gather x1, blocking collectives, per_device(): lax.all_gather(finished[0].astype(jnp.bfloat16), 'section', axis=1, tiled...  43.7 us
  transfers between devices with their start and end apart: 3, of which 3 were waited for; matrix products, arithmetic and copies ran while one was open for 4% of the time, Pallas kernels for 0%

commit v1 on v0

v1 whole, which is shorter than its diff:
```python
import math

import jax
import jax.numpy as jnp
from jax import lax
from jax.experimental import pallas as pl
from jax.experimental.pallas import tpu as pltpu
from jax.sharding import Mesh
from jax.sharding import PartitionSpec as P

HEADS = 6
HEAD = 128
CACHE_FR = 6
FRAME_TOK = 32
STEPS = 8
LANES = 128
QKV_BLOCKS = 18
KV_BLOCKS = 12
MSG_ROWS = 64
MOD_ROWS = 80
PLANE = ("x", "y", "c")
LINE = ("s", "w")
VMEM_LIMIT = 40 * 1024 * 1024

bf16 = jnp.bfloat16
f32 = jnp.float32


def product(left, right):
    return jnp.dot(left, right, preferred_element_type=f32)


def product_t(left, right):
    return lax.dot_general(left, right, (((1,), (1,)), ((), ())), preferred_element_type=f32)


def sinusoid(time_values, freq_count):
    half_count = freq_count // 2
    frequency = jnp.exp(-math.log(10000.0) * jnp.arange(half_count, dtype=f32) / half_count)
    phase_grid = time_values.astype(f32)[:, None] * frequency[None, :]
    return jnp.concatenate([jnp.cos(phase_grid), jnp.sin(phase_grid)], axis=1)


def pack_line(w_qkv_ref, finished_ref, embed_ref, w_time_ref, out_ref, held):
    rows = w_qkv_ref[...].astype(f32)
    for block in range(QKV_BLOCKS):
        held[3 * block : 3 * block + 3, :] = rows[:, block * LANES : (block + 1) * LANES]
    tokens = finished_ref[...].astype(bf16).astype(f32).T
    held[54:60, 0:64] = tokens[0:6]
    held[54:60, 64:128] = tokens[6:12]
    embed = embed_ref[...]
    w_time = w_time_ref[...]
    first = embed.astype(bf16)
    rest = embed - first.astype(f32)
    second = rest.astype(bf16)
    third = (rest - second.astype(f32)).astype(bf16)
    mods = product(first, w_time) + (product(second, w_time) + product(third, w_time))
    coarse = mods.astype(bf16).astype(f32)
    fine = mods - coarse
    held[60:64, :] = jnp.zeros((4, LANES), f32)
    held[62:63, 0:120] = coarse[STEPS : STEPS + 1]
    held[63:64, 0:120] = fine[STEPS : STEPS + 1]
    common = held[0:48, :].astype(bf16)
    for section in range(STEPS):
        step = (section - 1) % STEPS
        held[60:61, 0:120] = coarse[step : step + 1]
        held[61:62, 0:120] = fine[step : step + 1]
        last = held[48:64, :].astype(bf16)
        for side in range(2):
            out_ref[2 * section + side, 0:48, :] = common
            out_ref[2 * section + side, 48:64, :] = last


def pack_plane(side_ref, got_ref, out_ref, finished_ref, wide, tokens):
    side = side_ref[0]
    for peer in range(16):
        wide[peer * MSG_ROWS : (peer + 1) * MSG_ROWS, :] = got_ref[peer].astype(f32)
    for block in range(QKV_BLOCKS):
        for row in range(3):
            piece = wide[pl.ds(3 * block + row, 16, stride=MSG_ROWS), :].astype(bf16)
            out_ref[block, 16 * row : 16 * row + 16, :] = piece
            if block >= QKV_BLOCKS - KV_BLOCKS:
                out_ref[block + KV_BLOCKS, 16 * row : 16 * row + 16, :] = piece
            if block == QKV_BLOCKS - 1:
                out_ref[30, 16 * row : 16 * row + 16, :] = piece
                out_ref[31, 16 * row : 16 * row + 16, :] = piece
    mods = jnp.concatenate(
        [wide[60:64, :], wide[MSG_ROWS + 60 : MSG_ROWS + 64, :], jnp.zeros((8, LANES), f32)], axis=0
    ).astype(bf16)
    for target in range(32):
        out_ref[target, 48:64, :] = mods
    for section in range(STEPS):
        piece = wide[pl.ds(section * 2 * MSG_ROWS + side * MSG_ROWS + 54, 6), :]
        tokens[6 * section : 6 * section + 6, :] = piece[:, 0:64]
        tokens[48 + 6 * section : 54 + 6 * section, :] = piece[:, 64:128]
    finished_ref[...] = tokens[...].astype(bf16)


def flatten_mods(wide, kind, flat):
    groups = []
    for x in range(4):
        for w in range(2):
            begin = x * 8 * MSG_ROWS + 48 + w * 4 + 2 * kind
            groups.append(
                wide[pl.ds(begin, 8, stride=MSG_ROWS), :]
                + wide[pl.ds(begin + 1, 8, stride=MSG_ROWS), :]
            )
    runs = jnp.concatenate(groups, axis=0)
    place = lax.broadcasted_iota(jnp.int32, (64, LANES), 0) % 16
    lane = lax.broadcasted_iota(jnp.int32, (64, LANES), 1)
    for bit in range(4):
        turned = pltpu.roll(runs, LANES - 8 * 2**bit, axis=1)
        runs = jnp.where((place & 2**bit) != 0, turned, runs)
    runs = jnp.where(lane < 120 - 8 * place, runs, pltpu.roll(runs, 63, axis=0))
    for quarter in range(4):
        flat[15 * quarter : 15 * quarter + 15, :] = runs[16 * quarter : 16 * quarter + 15]
    flat[60:64, :] = jnp.zeros((4, LANES), f32)


def fold_block(block_ref, got_ref, w_in_ref, out_ref, mods_ref, wide, rows, scaled, flat_own, flat_rest):
    for peer in range(32):
        wide[peer * MSG_ROWS : (peer + 1) * MSG_ROWS, :] = got_ref[peer].astype(f32)
    for s in range(STEPS):
        for x in range(4):
            for w in range(2):
                for row in range(3):
                    rows[pl.ds(((s * 4 + x) * 2 + w) * 24 + row, 8, stride=3), :] = wide[
                        pl.ds(x * 8 * MSG_ROWS + row * 16 + s * 2 + w, 8, stride=MSG_ROWS), :
                    ]
    flatten_mods(wide, 0, flat_own)
    flatten_mods(wide, 1, flat_rest)
    mods_ref[...] = flat_own[...]
    at_rest = block_ref[0] >= QKV_BLOCKS
    used = jnp.where(at_rest, flat_rest[0:24, :], flat_own[0:24, :])
    turned = jnp.concatenate([used, jnp.zeros((LANES - 24, LANES), f32)], axis=0).T
    constant = jnp.zeros((8, LANES), f32)
    for part in range(12):
        piece = rows[part * LANES : (part + 1) * LANES, :]
        scaled[part * LANES : (part + 1) * LANES, :] = (
            piece * (1.0 + turned[:, 12 + part : 13 + part])
        ).astype(bf16)
        constant = constant + jnp.sum(
            (piece * turned[:, part : part + 1]).reshape(16, 8, LANES), axis=0
        )
    constant = jnp.sum(constant, axis=0, keepdims=True)
    w_in = w_in_ref[...]
    left = jnp.concatenate([w_in, jnp.ones((16, w_in.shape[1]), bf16)], axis=0)
    raw = product(left, scaled[...])
    middle = jnp.mean(w_in.astype(f32), axis=1, keepdims=True)
    linear = (raw[0:64] - middle * raw[64:65]).astype(bf16)
    coarse = constant.astype(bf16).astype(f32)
    tail = jnp.concatenate([coarse, constant - coarse, jnp.zeros((14, LANES), f32)], axis=0).astype(bf16)
    for target in range(32):
        out_ref[target, 0:64, :] = linear
        out_ref[target, 64:80, :] = tail


def spread_of(values):
    middle = jnp.mean(values, axis=-1, keepdims=True)
    centered = values - middle
    return centered, lax.rsqrt(jnp.mean(centered * centered, axis=-1, keepdims=True) + 1e-06)


def finish(
    window_ref,
    sigma_ref,
    got_ref,
    tokens_ref,
    state_ref,
    keys_ref,
    values_ref,
    mods_ref,
    w_in_ref,
    wo_ref,
    w_out_ref,
    out_ref,
    projected,
    mixture,
    after,
):
    current = state_ref[0:64, :]
    noise = state_ref[64:128, :]
    w_in = w_in_ref[...]
    tokens = current.T.astype(bf16)
    hidden = product(tokens, w_in)
    _, root = spread_of(hidden)
    done = tokens_ref[...]
    _, done_root = spread_of(product(done, w_in))

    def project(rows, factor, block):
        tail = got_ref[block, 64:80, :].astype(f32)
        return (product(rows, got_ref[block, 0:64, :]) * factor + (tail[0:1] + tail[1:2])).astype(bf16)

    start = window_ref[0]
    count = window_ref[1]
    frame = lax.broadcasted_iota(jnp.int32, (1, CACHE_FR * FRAME_TOK), 1) // FRAME_TOK
    frame = frame - start
    frame = jnp.where(frame < 0, frame + CACHE_FR, frame)
    bias = jnp.where(frame < count, 0.0, -jnp.inf)
    factor = 1.0 / math.sqrt(HEAD)
    for head in range(HEADS):
        columns = slice(head * HEAD, (head + 1) * HEAD)
        query = project(tokens, root, head)
        own_key = project(tokens, root, HEADS + head)
        own_value = project(tokens, root, 2 * HEADS + head)
        done_key = project(done, done_root, 3 * HEADS + head)
        done_value = project(done, done_root, 4 * HEADS + head)
        held = product_t(query, keys_ref[:, columns]) * factor + bias
        own = product_t(query, own_key) * factor
        last = product_t(query, done_key) * factor
        highest = jnp.maximum(
            jnp.max(held, axis=-1, keepdims=True),
            jnp.maximum(jnp.max(own, axis=-1, keepdims=True), jnp.max(last, axis=-1, keepdims=True)),
        )
        held = jnp.exp(held - highest)
        own = jnp.exp(own - highest)
        last = jnp.exp(last - highest)
        total = (
            jnp.sum(held, axis=-1, keepdims=True)
            + jnp.sum(own, axis=-1, keepdims=True)
            + jnp.sum(last, axis=-1, keepdims=True)
        )
        share = 1.0 / total
        mixture[:, columns] = (
            product((held * share).astype(bf16), values_ref[:, columns])
            + product((own * share).astype(bf16), own_value)
            + product((last * share).astype(bf16), done_value)
        ).astype(bf16)
    mixed = mixture[...]
    sums = jnp.zeros((tokens.shape[0], LANES), f32)
    for part in range(12):
        columns = slice(part * LANES, (part + 1) * LANES)
        attended = product_t(mixed, wo_ref[columns, :])
        value = hidden[:, columns] + mods_ref[24 + part : 25 + part, :] * attended
        after[:, columns] = value
        sums = sums + value
    width = 12 * LANES
    middle = jnp.sum(sums, axis=-1, keepdims=True) * (1.0 / width)
    sums = jnp.zeros((tokens.shape[0], LANES), f32)
    for part in range(12):
        columns = slice(part * LANES, (part + 1) * LANES)
        value = after[:, columns] - middle
        sums = sums + value * value
    root = lax.rsqrt(jnp.sum(sums, axis=-1, keepdims=True) * (1.0 / width) + 1e-06)
    for part in range(12):
        columns = slice(part * LANES, (part + 1) * LANES)
        value = (after[:, columns] - middle) * root
        projected[:, columns] = (
            value * (1.0 + mods_ref[48 + part : 49 + part, :]) + mods_ref[36 + part : 37 + part, :]
        ).astype(bf16)
    velocity = product(projected[...], w_out_ref[...]).T
    sigma_now = sigma_ref[0]
    sigma_next = sigma_ref[1]
    out_ref[...] = (1.0 - sigma_next) * (current - sigma_now * velocity) + sigma_next * noise


def whole(count):
    return [pl.BlockSpec(memory_space=pltpu.VMEM)] * count


def scalars(count):
    return [pl.BlockSpec(memory_space=pltpu.SMEM)] * count


def per_device(
    latents,
    renoise,
    finished,
    cache_keys,
    cache_values,
    window_start,
    window_count,
    timesteps,
    w_in,
    w_time,
    w_qkv,
    wo_rows,
    w_out,
):
    section = lax.axis_index("s")
    step = (section + STEPS - 1) % STEPS
    params = pltpu.CompilerParams(vmem_limit_bytes=VMEM_LIMIT)

    state = jnp.concatenate([latents[0, 0], renoise[0, 0]], axis=0)
    state = lax.ppermute(state, "s", [(i, (i + 1) % STEPS) for i in range(STEPS)])
    wo_all = lax.all_gather(wo_rows, ("x", "w", "y", "c"), axis=0, tiled=True)

    times = jnp.concatenate([timesteps, jnp.zeros((STEPS,), jnp.int32)])
    embed = sinusoid(times, w_time.shape[0])
    message = pl.pallas_call(
        pack_line,
        out_shape=jax.ShapeDtypeStruct((16, MSG_ROWS, LANES), bf16),
        in_specs=whole(4),
        out_specs=pl.BlockSpec(memory_space=pltpu.VMEM),
        scratch_shapes=[pltpu.VMEM((MSG_ROWS, LANES), f32)],
        compiler_params=params,
        name="pack_line",
    )(w_qkv, finished[0], embed, w_time)
    got = lax.all_to_all(message, LINE, 0, 0, tiled=True)

    side = lax.axis_index("w").astype(jnp.int32)[None]
    message, tokens = pl.pallas_call(
        pack_plane,
        out_shape=[
            jax.ShapeDtypeStruct((32, MSG_ROWS, LANES), bf16),
            jax.ShapeDtypeStruct((96, 64), bf16),
        ],
        in_specs=scalars(1) + whole(1),
        out_specs=whole(2),
        scratch_shapes=[pltpu.VMEM((16 * MSG_ROWS, LANES), f32), pltpu.VMEM((96, 64), f32)],
        compiler_params=params,
        name="pack_plane",
    )(side, got)
    got = lax.all_to_all(message, PLANE, 0, 0, tiled=True)

    block = lax.axis_index(PLANE).astype(jnp.int32)[None]
    message, mods = pl.pallas_call(
        fold_block,
        out_shape=[
            jax.ShapeDtypeStruct((32, MOD_ROWS, LANES), bf16),
            jax.ShapeDtypeStruct((64, LANES), f32),
        ],
        in_specs=scalars(1) + whole(2),
        out_specs=whole(2),
        scratch_shapes=[
            pltpu.VMEM((32 * MSG_ROWS, LANES), f32),
            pltpu.VMEM((1536, LANES), f32),
            pltpu.VMEM((1536, LANES), bf16),
            pltpu.VMEM((64, LANES), f32),
            pltpu.VMEM((64, LANES), f32),
        ],
        compiler_params=params,
        name="fold_block",
    )(block, got, w_in)
    got = lax.all_to_all(message, PLANE, 0, 0, tiled=True)

    time_now = timesteps[step]
    time_next = jnp.where(step + 1 < STEPS, timesteps[jnp.minimum(step + 1, STEPS - 1)], 0)
    sigma = jnp.stack([time_now, time_next]).astype(f32) / 1000.0
    window = jnp.concatenate([window_start, window_count])
    stepped = pl.pallas_call(
        finish,
        out_shape=jax.ShapeDtypeStruct((64, 96), f32),
        in_specs=scalars(2) + whole(9),
        out_specs=pl.BlockSpec(memory_space=pltpu.VMEM),
        scratch_shapes=[
            pltpu.VMEM((96, 1536), bf16),
            pltpu.VMEM((96, 768), bf16),
            pltpu.VMEM((96, 1536), f32),
        ],
        compiler_params=params,
        name="finish",
    )(window, sigma, got, tokens, state, cache_keys[0], cache_values[0], mods, w_in, wo_all, w_out)
    return stepped[None, None]


def solution(mesh):
    grid = Mesh(mesh.devices.reshape(8, 4, 2, 4, 2), ("s", "x", "w", "y", "c"))
    streams = ("x", "w", "y", "c")
    in_specs = (
        P("s", streams, None, None),
        P("s", streams, None, None),
        P(streams, None, "s"),
        P(streams, None, None),
        P(streams, None, None),
        P(streams),
        P(streams),
        P(),
        P(),
        P(None, streams),
        P(("s",) + streams, None),
        P(streams, None),
        P(),
    )
    out_specs = P("s", streams, None, None)
    return jax.shard_map(
        per_device, mesh=grid, in_specs=in_specs, out_specs=out_specs, check_vma=False
    )
```

time: 981 us -> 151 us (0.15)
  waiting for transfers between devices: 704 us -> 81.5 us
  blocking collectives: 212 us -> 0 us
  starting transfers between devices: 1.96 us -> 37 us
  local copies, waits for them, and re-layouts: 24.3 us -> 5 us
  matrix products: 13.3 us -> 0 us
  Pallas kernels: 0 us -> 10.3 us
    all_gather x2 -> x1, waiting for transfers between devices: 693 us -> 49.6 us  [per_device(): wo_all = lax.all_gather(wo_rows, ('x', 'w', 'y', 'c'), axis=0, tiled=True)]
    all_gather x2 -> x0, blocking collectives: 212 us -> none  [the longest x1 168 us: per_device(): modulation = lax.all_gather(local_mod, 'mp', axis=1, tiled=True)]
    all_to_all x0 -> x3, starting transfers between devices: none -> 31.3 us  [the longest x1 15.9 us: per_device(): got = lax.all_to_all(message, LINE, 0, 0, tiled=True)]
    all_to_all x0 -> x3, waiting for transfers between devices: none -> 28.5 us  [the longest x1 16 us: per_device(): got = lax.all_to_all(message, LINE, 0, 0, tiled=True)]
    unnamed x17 -> x21, local copies, waits for them, and re-layouts: 18.7 us -> 4.36 us
    dot_general x19 -> x0, matrix products: 13.3 us -> none  [the longest x1 3.42 us: add_rows(): jnp.dot(done_rows, segment[:, inner_width:], preferred_element_type=jnp.f...]
    pallas_call x0 -> x4, Pallas kernels: none -> 10.3 us  [the longest x1 6.07 us: per_device(): pl.pallas_call(finish, out_shape=jax.ShapeDtypeStruct((64, 96), f32), in_...]
  transfers between devices with their start and end apart: 3 -> 5, of which waited for: 3 -> 5; matrix products, arithmetic and copies ran while one was open for 4% -> 3% of each run, Pallas kernels for 0% -> 3%
where the time goes in v1:
time: 151 us
  waiting for transfers between devices  81.5 us (54%)
  starting transfers between devices  37 us (25%)
  between operations  15.5 us (10%)
  Pallas kernels  10.3 us (7%)
  local copies, waits for them, and re-layouts  5 us (3%)
  other arithmetic  1.6 us (1%)
    all_gather x1, waiting for transfers between devices, per_device(): wo_all = lax.all_gather(wo_rows, ('x', 'w', 'y', 'c'), axis=0, tiled=True)  49.6 us
    all_to_all x1, waiting for transfers between devices, per_device(): got = lax.all_to_all(message, LINE, 0, 0, tiled=True)  16 us
    all_to_all x1, starting transfers between devices, per_device(): got = lax.all_to_all(message, LINE, 0, 0, tiled=True)  15.9 us
    all_to_all x2, starting transfers between devices, per_device(): got = lax.all_to_all(message, PLANE, 0, 0, tiled=True)  15.5 us
    all_to_all x2, waiting for transfers between devices, per_device(): got = lax.all_to_all(message, PLANE, 0, 0, tiled=True)  12.5 us
    pallas_call x1, Pallas kernels, per_device(): pl.pallas_call(finish, out_shape=jax.ShapeDtypeStruct((64, 96), f32), in_...  6.07 us
    ppermute x1, starting transfers between devices, per_device(): lax.ppermute(state, 's', [(i, (i + 1) % STEPS) for i in range(STEPS)])  5.69 us
    unnamed x21, local copies, waits for them, and re-layouts  4.36 us
  transfers between devices with their start and end apart: 5, of which 5 were waited for; matrix products, arithmetic and copies ran while one was open for 3% of the time, Pallas kernels for 3%

profile of v1, /device:TPU:1, one launch (start us, length us, event | category | flops | bytes accessed | tf_op | source)
XLA Modules:
  0.0 150.8 jit_solution(5732089146691416465)
XLA Ops:
  6.5 0.0 copy-start.1
  6.5 0.0 copy-start.7
  6.5 0.0 copy-start.6
  6.5 0.0 all-gather.2.cloned.1.call-start
  6.5 0.7 all-gather.2.cloned.1.call-update
  7.3 0.9 copy.15.w_time_ref
  8.2 0.8 copy.14
  9.0 0.7 pad_convert_fusion
  9.7 0.1 multiply_cosine_fusion
  9.8 0.0 copy-start.4
  9.8 0.7 copy-done.4
  10.5 0.0 copy-start.8
  10.5 0.0 copy-start.5
  10.5 0.9 pack_line.1
  11.4 0.0 copy-start.2
  11.4 0.0 copy-start.3
  11.4 15.9 %all-to-all-start = ((bf16[16,64,128]{2,1,0:T(8,128)(2,1)}), bf16[16,64,128]{2,1,0:T(8,128)(2,1)S(1)}, u32[]{:S(2)}, u32[]{:S(2)}) async-start(bf16[16,64,128]{2,1,0:T(8,128)(2,1)} %pack_line.1), calls=%async_computation | async-start | bytes 524288 | tf_op jit(solution)/shard_map/all_to_all | solution.py:299
  27.3 16.0 %all-to-all-done.got_ref = bf16[16,64,128]{2,1,0:T(8,128)(2,1)S(1)} async-done(((bf16[16,64,128]{2,1,0:T(8,128)(2,1)}), bf16[16,64,128]{2,1,0:T(8,128)(2,1)S(1)}, u32[]{:S(2)}, u32[]{:S(2)}) %all-to-all-start) | async-done | bytes 262176 | tf_op jit(solution)/shard_map/all_to_all | solution.py:299
  43.3 1.1 pack_plane.1
  44.4 11.8 %all-to-all-start.1 = ((bf16[32,64,128]{2,1,0:T(8,128)(2,1)}), bf16[32,64,128]{2,1,0:T(8,128)(2,1)S(1)}, u32[]{:S(2)}, u32[]{:S(2)}) async-start(bf16[32,64,128]{2,1,0:T(8,128)(2,1)} %get-tuple-element.9), calls=%async_computation.1 | async-start | bytes 1048576 | tf_op jit(solution)/shard_map/all_to_all | solution.py:314
  56.2 11.6 %all-to-all-done.1.got_ref = bf16[32,64,128]{2,1,0:T(8,128)(2,1)S(1)} async-done(((bf16[32,64,128]{2,1,0:T(8,128)(2,1)}), bf16[32,64,128]{2,1,0:T(8,128)(2,1)S(1)}, u32[]{:S(2)}, u32[]{:S(2)}) %all-to-all-start.1) | async-done | bytes 524320 | tf_op jit(solution)/shard_map/all_to_all | solution.py:314
  67.8 0.0 copy-done.1
  67.8 2.2 %fold_block.1 = (bf16[32,80,128]{2,1,0:T(8,128)(2,1)}, f32[64,128]{1,0:T(8,128)S(1)}) custom-call(s32[1]{0:T(128)} %bitcast.2.block_ref, bf16[32,64,128]{2,1,0:T(8,128)(2,1)S(1)} %all-to-all-done.1.got_ref, bf16[64,1536]{1,0:T(8,128)(2,1)S(1)} %copy-done.1), custom_call_target="tpu_custom_call" | custom-call | tf_op jit(solution)/shard_map/fold_block/pallas_call | solution.py:317
  70.0 3.7 %all-to-all-start.2 = ((bf16[32,80,128]{2,1,0:T(8,128)(2,1)}), bf16[32,80,128]{2,1,0:T(8,128)(2,1)S(1)}, u32[]{:S(2)}, u32[]{:S(2)}) async-start(bf16[32,80,128]{2,1,0:T(8,128)(2,1)} %get-tuple-element.10), calls=%async_computation.2 | async-start | bytes 1310720 | tf_op jit(solution)/shard_map/all_to_all | solution.py:335
  73.7 0.0 copy-done.7
  73.7 0.0 copy-done.6
  73.7 5.7 %collective-permute-start = (f32[128,96]{1,0:T(8,128)S(1)}, f32[128,96]{1,0:T(8,128)S(1)}, u32[]{:S(2)}, u32[]{:S(2)}) collective-permute-start(f32[128,96]{1,0:T(8,128)S(1)} %pad_maximum_fusion), channel_id=1, source_target_pairs={{0,64},{64,128},{128,192},{192,256},{256,320},{320,384},{384,448},... | collective-permute-start | bytes 147464 | tf_op jit(solution)/shard_map/ppermute | solution.py:285
  80.8 0.0 copy-done.8
  80.8 0.6 fusion.1
  82.0 0.7 fusion.sigma_ref
  82.8 0.1 pad_add_fusion.window_ref
  82.8 0.0 copy-done.5
  82.8 0.2 copy.16.w_out_ref
  83.1 2.7 %collective-permute-done.state_ref = f32[128,96]{1,0:T(8,128)S(1)} collective-permute-done((f32[128,96]{1,0:T(8,128)S(1)}, f32[128,96]{1,0:T(8,128)S(1)}, u32[]{:S(2)}, u32[]{:S(2)}) %collective-permute-start) | collective-permute-done | bytes 49184 | tf_op jit(solution)/shard_map/ppermute | solution.py:285
  85.8 0.9 all-to-all-done.2.got_ref
  86.7 49.6 %all-gather.2.cloned.1.call-done.wo_ref = bf16[1536,768]{1,0:T(8,128)(2,1)} async-done(((bf16[24,768]{1,0:T(8,128)(2,1)}), bf16[1536,768]{1,0:T(8,128)(2,1)}) %all-gather.2.cloned.1.call-update) | async-done | bytes 2359312 | tf_op jit(solution)/shard_map/all_gather | solution.py:286
  136.2 0.0 copy-done.2
  136.2 0.0 copy-done.3
  136.2 0.0 copy-start
  136.2 1.7 %copy-done = bf16[1536,768]{1,0:T(8,128)(2,1)S(1)} copy-done((bf16[1536,768]{1,0:T(8,128)(2,1)S(1)}, bf16[1536,768]{1,0:T(8,128)(2,1)}, u32[]{:S(2)}) %copy-start) | copy-done | bytes 2359320
  137.9 6.1 %finish.1 = f32[64,96]{1,0:T(8,128)} custom-call(s32[2]{0:T(128)S(1)} %pad_add_fusion.window_ref, f32[2]{0:T(128)S(1)} %fusion.sigma_ref, bf16[32,80,128]{2,1,0:T(8,128)(2,1)S(1)} %all-to-all-done.2.got_ref, bf16[96,64]{1,0:T(8,128)(2,1)S(1)} %get-tuple-element.11.tokens_ref, f32[128,96]{1,0:T(8,128)S(1)} %collective-permute-done.state_ref, ...), custom_call_target="tpu_custom_call" | custom-call | tf_op jit(solution)/shard_map/finish/pallas_call | solution.py:341
  (3 shorter events, 0.0 us)
Async XLA Ops:
  6.5 61.3 %copy-start.1 = (bf16[64,1536]{1,0:T(8,128)(2,1)S(1)}, bf16[64,1536]{1,0:T(8,128)(2,1)}, u32[]{:S(2)}) copy-start(bf16[64,1536]{1,0:T(8,128)(2,1)} %w_in_ref.3) | copy-start | bytes 589828
  6.5 67.2 %copy-start.7 = (f32[1,1,64,96]{3,2,1,0:T(8,128)S(1)}, f32[1,1,64,96]{3,2,1,0:T(8,128)}, u32[]{:S(2)}) copy-start(f32[1,1,64,96]{3,2,1,0:T(8,128)} %param.13) | copy-start | bytes 73732
  6.5 67.2 %copy-start.6 = (f32[1,1,64,96]{3,2,1,0:T(8,128)S(1)}, f32[1,1,64,96]{3,2,1,0:T(8,128)}, u32[]{:S(2)}) copy-start(f32[1,1,64,96]{3,2,1,0:T(8,128)} %param.14) | copy-start | bytes 73732
  6.5 129.7 %all-gather.2.cloned.1.call-start = ((), (), s32[]{:S(2)}) async-start(), calls=%async_computation.3 | async-start | bytes 2396160 | tf_op jit(solution)/shard_map/all_gather | solution.py:286
  9.8 0.7 copy-start.4
  10.5 70.2 %copy-start.8 = (s32[8]{0:T(128)S(1)}, s32[8]{0:T(128)}, u32[]{:S(2)}) copy-start(s32[8]{0:T(128)} %param.20) | copy-start | bytes 100
  10.5 72.3 %copy-start.5 = (bf16[1536,64]{0,1:T(8,128)(2,1)S(1)}, bf16[1536,64]{0,1:T(8,128)(2,1)}, u32[]{:S(2)}) copy-start(bf16[1536,64]{0,1:T(8,128)(2,1)} %param.25) | copy-start | bytes 589828
  11.4 124.8 %copy-start.2 = (bf16[1,192,768]{2,1,0:T(8,128)(2,1)S(1)}, bf16[1,192,768]{2,1,0:T(8,128)(2,1)}, u32[]{:S(2)}) copy-start(bf16[1,192,768]{2,1,0:T(8,128)(2,1)} %param.16) | copy-start | bytes 884740
  11.4 124.8 %copy-start.3 = (bf16[1,192,768]{2,1,0:T(8,128)(2,1)S(1)}, bf16[1,192,768]{2,1,0:T(8,128)(2,1)}, u32[]{:S(2)}) copy-start(bf16[1,192,768]{2,1,0:T(8,128)(2,1)} %param.17) | copy-start | bytes 884740
  11.4 31.9 %all-to-all-start = ((bf16[16,64,128]{2,1,0:T(8,128)(2,1)}), bf16[16,64,128]{2,1,0:T(8,128)(2,1)S(1)}, u32[]{:S(2)}, u32[]{:S(2)}) async-start(bf16[16,64,128]{2,1,0:T(8,128)(2,1)} %pack_line.1), calls=%async_computation | async-start | bytes 524288 | tf_op jit(solution)/shard_map/all_to_all | solution.py:299
  44.4 23.4 %all-to-all-start.1 = ((bf16[32,64,128]{2,1,0:T(8,128)(2,1)}), bf16[32,64,128]{2,1,0:T(8,128)(2,1)S(1)}, u32[]{:S(2)}, u32[]{:S(2)}) async-start(bf16[32,64,128]{2,1,0:T(8,128)(2,1)} %get-tuple-element.9), calls=%async_computation.1 | async-start | bytes 1048576 | tf_op jit(solution)/shard_map/all_to_all | solution.py:314
  70.0 16.7 %all-to-all-start.2 = ((bf16[32,80,128]{2,1,0:T(8,128)(2,1)}), bf16[32,80,128]{2,1,0:T(8,128)(2,1)S(1)}, u32[]{:S(2)}, u32[]{:S(2)}) async-start(bf16[32,80,128]{2,1,0:T(8,128)(2,1)} %get-tuple-element.10), calls=%async_computation.2 | async-start | bytes 1310720 | tf_op jit(solution)/shard_map/all_to_all | solution.py:335
  73.7 12.0 %collective-permute-start = (f32[128,96]{1,0:T(8,128)S(1)}, f32[128,96]{1,0:T(8,128)S(1)}, u32[]{:S(2)}, u32[]{:S(2)}) collective-permute-start(f32[128,96]{1,0:T(8,128)S(1)} %pad_maximum_fusion), channel_id=1, source_target_pairs={{0,64},{64,128},{128,192},{192,256},{256,320},{320,384},{384,448},... | collective-permute-start | bytes 147464 | tf_op jit(solution)/shard_map/ppermute | solution.py:285
  136.2 1.7 %copy-start = (bf16[1536,768]{1,0:T(8,128)(2,1)S(1)}, bf16[1536,768]{1,0:T(8,128)(2,1)}, u32[]{:S(2)}) copy-start(bf16[1536,768]{1,0:T(8,128)(2,1)} %all-gather.2.cloned.1.call-done.wo_ref) | copy-start | bytes 7077892
Sparse Core Ops, SparseCore 0:
  11.8 124.4 all-gather.1

commit v2 on v1

--- a/solution.py
+++ b/solution.py
@@ -16,11 +16,13 @@
 LANES = 128
 QKV_BLOCKS = 18
 KV_BLOCKS = 12
+LINE_ROWS = 88
 MSG_ROWS = 64
+PLANE_ROWS = 208
 MOD_ROWS = 80
 PLANE = ("x", "y", "c")
 LINE = ("s", "w")
-VMEM_LIMIT = 40 * 1024 * 1024
+VMEM_LIMIT = 16 * 1024 * 1024
 
 bf16 = jnp.bfloat16
 f32 = jnp.float32
@@ -34,33 +36,48 @@
     return lax.dot_general(left, right, (((1,), (1,)), ((), ())), preferred_element_type=f32)
 
 
-def sinusoid(time_values, freq_count):
-    half_count = freq_count // 2
-    frequency = jnp.exp(-math.log(10000.0) * jnp.arange(half_count, dtype=f32) / half_count)
-    phase_grid = time_values.astype(f32)[:, None] * frequency[None, :]
-    return jnp.concatenate([jnp.cos(phase_grid), jnp.sin(phase_grid)], axis=1)
-
-
-def pack_line(w_qkv_ref, finished_ref, embed_ref, w_time_ref, out_ref, held):
+def pack_line(times_ref, *refs):
+    out_ref, held, wo_held, w_qkv_ref, finished_ref, w_time_ref, wo_ref, arrived = refs[4:]
+    copies = [
+        pltpu.make_async_copy(source, target, arrived.at[place])
+        for place, (source, target) in enumerate(zip(refs[:4], refs[7:11]))
+    ]
+    for copy in copies:
+        copy.start()
+    place = lax.broadcasted_iota(jnp.int32, (16, LANES), 0)
+    times = jnp.zeros((16, LANES), f32)
+    for step in range(STEPS):
+        times = jnp.where(place == step, times_ref[step].astype(f32), times)
+    lane = lax.broadcasted_iota(jnp.int32, (16, LANES), 1).astype(f32)
+    phase = times * jnp.exp(-math.log(10000.0) * lane / LANES)
+    embed = jnp.concatenate([jnp.cos(phase), jnp.sin(phase)], axis=1)
+    for copy in copies:
+        copy.wait()
     rows = w_qkv_ref[...].astype(f32)
     for block in range(QKV_BLOCKS):
         held[3 * block : 3 * block + 3, :] = rows[:, block * LANES : (block + 1) * LANES]
-    tokens = finished_ref[...].astype(bf16).astype(f32).T
+    tokens = finished_ref[...].reshape(12, 64).astype(bf16).astype(f32)
     held[54:60, 0:64] = tokens[0:6]
     held[54:60, 64:128] = tokens[6:12]
-    embed = embed_ref[...]
     w_time = w_time_ref[...]
     first = embed.astype(bf16)
     rest = embed - first.astype(f32)
     second = rest.astype(bf16)
     third = (rest - second.astype(f32)).astype(bf16)
-    mods = product(first, w_time) + (product(second, w_time) + product(third, w_time))
+    mods = product_t(first, w_time) + (product_t(second, w_time) + product_t(third, w_time))
     coarse = mods.astype(bf16).astype(f32)
     fine = mods - coarse
     held[60:64, :] = jnp.zeros((4, LANES), f32)
     held[62:63, 0:120] = coarse[STEPS : STEPS + 1]
     held[63:64, 0:120] = fine[STEPS : STEPS + 1]
+    wo = wo_ref[...].astype(f32)
+    section = lax.axis_index("s")
+    for block in range(HEADS):
+        wo_held[24 * block : 24 * block + 24, :] = wo[:, block * LANES : (block + 1) * LANES]
+        held[64 + 3 * block : 67 + 3 * block, :] = wo_held[pl.ds(24 * block + 3 * section, 3), :]
+    held[82:88, :] = jnp.zeros((6, LANES), f32)
     common = held[0:48, :].astype(bf16)
+    wo_rows = held[64:88, :].astype(bf16)
     for section in range(STEPS):
         step = (section - 1) % STEPS
         held[60:61, 0:120] = coarse[step : step + 1]
@@ -69,15 +86,16 @@
         for side in range(2):
             out_ref[2 * section + side, 0:48, :] = common
             out_ref[2 * section + side, 48:64, :] = last
-
-
-def pack_plane(side_ref, got_ref, out_ref, finished_ref, wide, tokens):
-    side = side_ref[0]
+            out_ref[2 * section + side, 64:88, :] = wo_rows
+
+
+def pack_plane(got_ref, out_ref, finished_ref, wide, tokens, wo):
+    side = lax.axis_index("w")
     for peer in range(16):
-        wide[peer * MSG_ROWS : (peer + 1) * MSG_ROWS, :] = got_ref[peer].astype(f32)
+        wide[peer * LINE_ROWS : (peer + 1) * LINE_ROWS, :] = got_ref[peer].astype(f32)
     for block in range(QKV_BLOCKS):
         for row in range(3):
-            piece = wide[pl.ds(3 * block + row, 16, stride=MSG_ROWS), :].astype(bf16)
+            piece = wide[pl.ds(3 * block + row, 16, stride=LINE_ROWS), :].astype(bf16)
             out_ref[block, 16 * row : 16 * row + 16, :] = piece
             if block >= QKV_BLOCKS - KV_BLOCKS:
                 out_ref[block + KV_BLOCKS, 16 * row : 16 * row + 16, :] = piece
@@ -85,12 +103,20 @@
                 out_ref[30, 16 * row : 16 * row + 16, :] = piece
                 out_ref[31, 16 * row : 16 * row + 16, :] = piece
     mods = jnp.concatenate(
-        [wide[60:64, :], wide[MSG_ROWS + 60 : MSG_ROWS + 64, :], jnp.zeros((8, LANES), f32)], axis=0
+        [wide[60:64, :], wide[LINE_ROWS + 60 : LINE_ROWS + 64, :], jnp.zeros((8, LANES), f32)], axis=0
     ).astype(bf16)
+    for half in range(2):
+        for block in range(HEADS):
+            for row in range(3):
+                wo[pl.ds(144 * half + 24 * block + row, 8, stride=3), :] = wide[
+                    pl.ds(half * LINE_ROWS + 64 + 3 * block + row, 8, stride=2 * LINE_ROWS), :
+                ]
+    halves = [wo[144 * half : 144 * (half + 1), :].astype(bf16) for half in range(2)]
     for target in range(32):
         out_ref[target, 48:64, :] = mods
+        out_ref[target, 64:208, :] = halves[target % 2]
     for section in range(STEPS):
-        piece = wide[pl.ds(section * 2 * MSG_ROWS + side * MSG_ROWS + 54, 6), :]
+        piece = wide[pl.ds(section * 2 * LINE_ROWS + side * LINE_ROWS + 54, 6), :]
         tokens[6 * section : 6 * section + 6, :] = piece[:, 0:64]
         tokens[48 + 6 * section : 54 + 6 * section, :] = piece[:, 64:128]
     finished_ref[...] = tokens[...].astype(bf16)
@@ -117,9 +143,9 @@
     flat[60:64, :] = jnp.zeros((4, LANES), f32)
 
 
-def fold_block(block_ref, got_ref, w_in_ref, out_ref, mods_ref, wide, rows, scaled, flat_own, flat_rest):
+def fold_block(got_ref, w_in_ref, state_ref, out_ref, mods_ref, wide, rows, scaled, flat_own, flat_rest):
     for peer in range(32):
-        wide[peer * MSG_ROWS : (peer + 1) * MSG_ROWS, :] = got_ref[peer].astype(f32)
+        wide[peer * MSG_ROWS : (peer + 1) * MSG_ROWS, :] = got_ref[peer, 0:MSG_ROWS, :].astype(f32)
     for s in range(STEPS):
         for x in range(4):
             for w in range(2):
@@ -130,7 +156,7 @@
     flatten_mods(wide, 0, flat_own)
     flatten_mods(wide, 1, flat_rest)
     mods_ref[...] = flat_own[...]
-    at_rest = block_ref[0] >= QKV_BLOCKS
+    at_rest = lax.axis_index(PLANE) >= QKV_BLOCKS
     used = jnp.where(at_rest, flat_rest[0:24, :], flat_own[0:24, :])
     turned = jnp.concatenate([used, jnp.zeros((LANES - 24, LANES), f32)], axis=0).T
     constant = jnp.zeros((8, LANES), f32)
@@ -161,25 +187,67 @@
     return centered, lax.rsqrt(jnp.mean(centered * centered, axis=-1, keepdims=True) + 1e-06)
 
 
+def unpack_wo(got_ref, mods_ref, out_ref):
+    for pair in range(16):
+        first = got_ref[2 * pair, 64:208, :].astype(f32)
+        second = got_ref[2 * pair + 1, 64:208, :].astype(f32)
+        for block in range(HEADS):
+            rows = slice(24 * block, 24 * block + 24)
+            out_ref[48 * pair : 48 * pair + 48, block * LANES : (block + 1) * LANES] = jnp.concatenate(
+                [first[rows], second[rows]], axis=0
+            ).astype(bf16)
+
+
+def sigmas(times_ref):
+    step = lax.rem(lax.axis_index("s") + STEPS - 1, STEPS)
+    now = times_ref[step].astype(f32) * 0.001
+    after = times_ref[lax.rem(step + 1, STEPS)].astype(f32) * 0.001
+    return now, jnp.where(step == STEPS - 1, 0.0, after)
+
+
 def finish(
-    window_ref,
-    sigma_ref,
+    start_ref,
+    count_ref,
+    times_ref,
     got_ref,
+    held_refs,
+    wo_refs,
+    out_ref,
+    normed,
+    mixture,
+    after,
+    state_ref,
+    w_in_ref,
     tokens_ref,
-    state_ref,
     keys_ref,
     values_ref,
     mods_ref,
-    w_in_ref,
-    wo_ref,
     w_out_ref,
-    out_ref,
-    projected,
-    mixture,
-    after,
+    wo,
+    arrived,
 ):
+    near = (state_ref, w_in_ref, tokens_ref, keys_ref, values_ref, mods_ref, w_out_ref)
+    copies = [
+        pltpu.make_async_copy(source, target, arrived.at[place])
+        for place, (source, target) in enumerate(zip(held_refs, near))
+    ]
+    core = lax.axis_index("c")
+    for half, side in enumerate((core, 1 - core)):
+        for x in range(4):
+            begin = pl.multiple_of(384 * x + 192 * side, 192)
+            source, place = (wo_refs[0], x) if half == 0 else (wo_refs[1 + x // 2], x % 2)
+            copies.append(
+                pltpu.make_async_copy(
+                    source.at[192 * place : 192 * (place + 1)],
+                    wo.at[pl.ds(begin, 192)],
+                    arrived.at[len(copies)],
+                )
+            )
+    for copy in copies:
+        copy.start()
+    for copy in copies[:3]:
+        copy.wait()
     current = state_ref[0:64, :]
-    noise = state_ref[64:128, :]
     w_in = w_in_ref[...]
     tokens = current.T.astype(bf16)
     hidden = product(tokens, w_in)
@@ -191,13 +259,15 @@
         tail = got_ref[block, 64:80, :].astype(f32)
         return (product(rows, got_ref[block, 0:64, :]) * factor + (tail[0:1] + tail[1:2])).astype(bf16)
 
-    start = window_ref[0]
-    count = window_ref[1]
+    start = start_ref[0]
+    count = count_ref[0]
     frame = lax.broadcasted_iota(jnp.int32, (1, CACHE_FR * FRAME_TOK), 1) // FRAME_TOK
     frame = frame - start
     frame = jnp.where(frame < 0, frame + CACHE_FR, frame)
     bias = jnp.where(frame < count, 0.0, -jnp.inf)
     factor = 1.0 / math.sqrt(HEAD)
+    for copy in copies[3:5]:
+        copy.wait()
     for head in range(HEADS):
         columns = slice(head * HEAD, (head + 1) * HEAD)
         query = project(tokens, root, head)
@@ -227,10 +297,12 @@
             + product((last * share).astype(bf16), done_value)
         ).astype(bf16)
     mixed = mixture[...]
+    for copy in copies[5:]:
+        copy.wait()
     sums = jnp.zeros((tokens.shape[0], LANES), f32)
     for part in range(12):
         columns = slice(part * LANES, (part + 1) * LANES)
-        attended = product_t(mixed, wo_ref[columns, :])
+        attended = product_t(mixed, wo[columns, :])
         value = hidden[:, columns] + mods_ref[24 + part : 25 + part, :] * attended
         after[:, columns] = value
         sums = sums + value
@@ -245,13 +317,10 @@
     for part in range(12):
         columns = slice(part * LANES, (part + 1) * LANES)
         value = (after[:, columns] - middle) * root
-        projected[:, columns] = (
-            value * (1.0 + mods_ref[48 + part : 49 + part, :]) + mods_ref[36 + part : 37 + part, :]
-        ).astype(bf16)
-    velocity = product(projected[...], w_out_ref[...]).T
-    sigma_now = sigma_ref[0]
-    sigma_next = sigma_ref[1]
-    out_ref[...] = (1.0 - sigma_next) * (current - sigma_now * velocity) + sigma_next * noise
+        normed[:, columns] = (value * (1.0 + mods_ref[48 + part : 49 + part, :]) + mods_ref[36 + part : 37 + part, :]).astype(bf16)
+    velocity = product_t(w_out_ref[...], normed[...])
+    sigma_now, sigma_next = sigmas(times_ref)
+    out_ref[...] = (1.0 - sigma_next) * (current - sigma_now * velocity) + sigma_next * state_ref[64:128, :]
 
 
 def whole(count):
@@ -260,6 +329,23 @@
 
 def scalars(count):
     return [pl.BlockSpec(memory_space=pltpu.SMEM)] * count
+
+
+def anywhere(count):
+    return [pl.BlockSpec(memory_space=pltpu.HBM)] * count
+
+
+def in_hbm(array):
+    return pltpu.with_memory_space_constraint(array, pltpu.HBM)
+
+
+def in_vmem(array):
+    return pltpu.with_memory_space_constraint(array, pltpu.VMEM)
+
+
+def shifted(array, axis, by):
+    size = lax.axis_size(axis)
+    return lax.ppermute(array, axis, [(i, (i - by) % size) for i in range(size)])
 
 
 def per_device(
@@ -277,50 +363,53 @@
     wo_rows,
     w_out,
 ):
-    section = lax.axis_index("s")
-    step = (section + STEPS - 1) % STEPS
     params = pltpu.CompilerParams(vmem_limit_bytes=VMEM_LIMIT)
 
-    state = jnp.concatenate([latents[0, 0], renoise[0, 0]], axis=0)
-    state = lax.ppermute(state, "s", [(i, (i + 1) % STEPS) for i in range(STEPS)])
-    wo_all = lax.all_gather(wo_rows, ("x", "w", "y", "c"), axis=0, tiled=True)
-
-    times = jnp.concatenate([timesteps, jnp.zeros((STEPS,), jnp.int32)])
-    embed = sinusoid(times, w_time.shape[0])
     message = pl.pallas_call(
         pack_line,
-        out_shape=jax.ShapeDtypeStruct((16, MSG_ROWS, LANES), bf16),
-        in_specs=whole(4),
+        out_shape=pltpu.VMEM((16, LINE_ROWS, LANES), bf16),
+        in_specs=scalars(1) + anywhere(4),
         out_specs=pl.BlockSpec(memory_space=pltpu.VMEM),
-        scratch_shapes=[pltpu.VMEM((MSG_ROWS, LANES), f32)],
+        scratch_shapes=[
+            pltpu.VMEM((LINE_ROWS, LANES), f32),
+            pltpu.VMEM((144, LANES), f32),
+            pltpu.VMEM(w_qkv.shape, bf16),
+            pltpu.VMEM((12, 1, 64), f32),
+            pltpu.VMEM((120, 256), bf16),
+            pltpu.VMEM(wo_rows.shape, bf16),
+            pltpu.SemaphoreType.DMA((4,)),
+        ],
         compiler_params=params,
         name="pack_line",
-    )(w_qkv, finished[0], embed, w_time)
+    )(timesteps, *map(in_hbm, (w_qkv, jnp.transpose(finished, (2, 0, 1)), w_time.T, wo_rows)))
     got = lax.all_to_all(message, LINE, 0, 0, tiled=True)
 
-    side = lax.axis_index("w").astype(jnp.int32)[None]
+    state = shifted(jnp.concatenate([latents[0, 0], renoise[0, 0]], axis=0), "s", -1)
     message, tokens = pl.pallas_call(
         pack_plane,
         out_shape=[
-            jax.ShapeDtypeStruct((32, MSG_ROWS, LANES), bf16),
-            jax.ShapeDtypeStruct((96, 64), bf16),
-        ],
-        in_specs=scalars(1) + whole(1),
+            pltpu.VMEM((32, PLANE_ROWS, LANES), bf16),
+            pltpu.HBM((96, 64), bf16),
+        ],
+        in_specs=whole(1),
         out_specs=whole(2),
-        scratch_shapes=[pltpu.VMEM((16 * MSG_ROWS, LANES), f32), pltpu.VMEM((96, 64), f32)],
+        scratch_shapes=[
+            pltpu.VMEM((16 * LINE_ROWS, LANES), f32),
+            pltpu.VMEM((96, 64), f32),
+            pltpu.VMEM((288, LANES), f32),
+        ],
         compiler_params=params,
         name="pack_plane",
-    )(side, got)
+    )(in_vmem(got))
     got = lax.all_to_all(message, PLANE, 0, 0, tiled=True)
 
-    block = lax.axis_index(PLANE).astype(jnp.int32)[None]
     message, mods = pl.pallas_call(
         fold_block,
         out_shape=[
-            jax.ShapeDtypeStruct((32, MOD_ROWS, LANES), bf16),
-            jax.ShapeDtypeStruct((64, LANES), f32),
-        ],
-        in_specs=scalars(1) + whole(2),
+            pltpu.VMEM((32, MOD_ROWS, LANES), bf16),
+            pltpu.HBM((64, LANES), f32),
+        ],
+        in_specs=whole(2) + anywhere(1),
         out_specs=whole(2),
         scratch_shapes=[
             pltpu.VMEM((32 * MSG_ROWS, LANES), f32),
@@ -331,26 +420,49 @@
         ],
         compiler_params=params,
         name="fold_block",
-    )(block, got, w_in)
+    )(in_vmem(got), w_in, in_hbm(state))
+    wo_half = pl.pallas_call(
+        unpack_wo,
+        out_shape=pltpu.VMEM((768, 768), bf16),
+        in_specs=whole(1) + anywhere(1),
+        out_specs=pl.BlockSpec(memory_space=pltpu.VMEM),
+        compiler_params=params,
+        name="unpack_wo",
+    )(in_vmem(got), in_hbm(mods))
+    wo_other = [shifted(wo_half[384 * part : 384 * (part + 1)], "c", 1) for part in range(2)]
     got = lax.all_to_all(message, PLANE, 0, 0, tiled=True)
 
-    time_now = timesteps[step]
-    time_next = jnp.where(step + 1 < STEPS, timesteps[jnp.minimum(step + 1, STEPS - 1)], 0)
-    sigma = jnp.stack([time_now, time_next]).astype(f32) / 1000.0
-    window = jnp.concatenate([window_start, window_count])
     stepped = pl.pallas_call(
-        finish,
+        lambda *refs: finish(*refs[:4], refs[4:11], refs[11:14], *refs[14:]),
         out_shape=jax.ShapeDtypeStruct((64, 96), f32),
-        in_specs=scalars(2) + whole(9),
+        in_specs=scalars(3) + whole(1) + anywhere(10),
         out_specs=pl.BlockSpec(memory_space=pltpu.VMEM),
         scratch_shapes=[
             pltpu.VMEM((96, 1536), bf16),
             pltpu.VMEM((96, 768), bf16),
             pltpu.VMEM((96, 1536), f32),
+            pltpu.VMEM((128, 96), f32),
+            pltpu.VMEM((64, 1536), bf16),
+            pltpu.VMEM((96, 64), bf16),
+            pltpu.VMEM((192, 768), bf16),
+            pltpu.VMEM((192, 768), bf16),
+            pltpu.VMEM((64, LANES), f32),
+            pltpu.VMEM((64, 1536), bf16),
+            pltpu.VMEM((1536, 768), bf16),
+            pltpu.SemaphoreType.DMA((15,)),
         ],
         compiler_params=params,
         name="finish",
-    )(window, sigma, got, tokens, state, cache_keys[0], cache_values[0], mods, w_in, wo_all, w_out)
+    )(
+        window_start,
+        window_count,
+        timesteps,
+        in_vmem(got),
+        *map(
+            in_hbm,
+            (state, w_in, tokens, cache_keys[0], cache_values[0], mods, w_out.T, wo_half, *wo_other),
+        ),
+    )
     return stepped[None, None]
 
 

time: 151 us -> 103 us (0.68)
  waiting for transfers between devices: 81.5 us -> 25.7 us
  blocking collectives: 0 us -> 34.9 us
  between operations: 15.5 us -> 1.43 us
  starting transfers between devices: 37 us -> 26.1 us
  local copies, waits for them, and re-layouts: 5 us -> 0.77 us
  Pallas kernels: 10.3 us -> 13.1 us
  other arithmetic: 1.6 us -> 0.01 us
    all_gather x1 -> x0, waiting for transfers between devices: 49.6 us -> none  [per_device(): wo_all = lax.all_gather(wo_rows, ('x', 'w', 'y', 'c'), axis=0, tiled=True)]
    all_to_all x0 -> x1, blocking collectives: none -> 34.9 us  [per_device(): got = lax.all_to_all(message, LINE, 0, 0, tiled=True)]
    all_to_all x1 -> x0, waiting for transfers between devices: 16 us -> none  [per_device(): got = lax.all_to_all(message, LINE, 0, 0, tiled=True)]
    all_to_all x1 -> x0, starting transfers between devices: 15.9 us -> none  [per_device(): got = lax.all_to_all(message, LINE, 0, 0, tiled=True)]
    all_to_all x2, waiting for transfers between devices: 12.5 us -> 18.6 us  [per_device(): got = lax.all_to_all(message, PLANE, 0, 0, tiled=True)]
    ppermute x1 -> x3, waiting for transfers between devices: 2.7 us -> 7.05 us  [shifted(): lax.ppermute(array, axis, [(i, (i - by) % size) for i in range(size)])]
    ppermute x1 -> x3, starting transfers between devices: 5.69 us -> 9.74 us  [shifted(): lax.ppermute(array, axis, [(i, (i - by) % size) for i in range(size)])]
    unnamed x21 -> x18, local copies, waits for them, and re-layouts: 4.36 us -> 0.69 us
  transfers between devices with their start and end apart: 5 -> 5, of which waited for: 5 -> 4; matrix products, arithmetic and copies ran while one was open for 3% -> 0% of each run, Pallas kernels for 3% -> 0%
where the time goes in v2:
time: 103 us; the launch traced here: 102 us
  blocking collectives  34.9 us (34%)
  starting transfers between devices  26.1 us (25%)
  waiting for transfers between devices  25.7 us (25%)
  Pallas kernels  13.1 us (13%)
  between operations  1.43 us (1%)
    all_to_all x1, blocking collectives, per_device(): got = lax.all_to_all(message, LINE, 0, 0, tiled=True)  34.9 us
    all_to_all x2, waiting for transfers between devices, per_device(): got = lax.all_to_all(message, PLANE, 0, 0, tiled=True)  18.6 us
    all_to_all x2, starting transfers between devices, per_device(): got = lax.all_to_all(message, PLANE, 0, 0, tiled=True)  16.3 us
    ppermute x3, starting transfers between devices, shifted(): lax.ppermute(array, axis, [(i, (i - by) % size) for i in range(size)])  9.74 us
    pallas_call x1, Pallas kernels, per_device(): pl.pallas_call(lambda *refs: finish(*refs[:4], refs[4:11], refs[11:14], *...  7.49 us
    ppermute x3, waiting for transfers between devices, shifted(): lax.ppermute(array, axis, [(i, (i - by) % size) for i in range(size)])  7.05 us
    pallas_call x1, Pallas kernels, per_device(): pl.pallas_call(fold_block, out_shape=[pltpu.VMEM((32, MOD_ROWS, LANES), b...  2.21 us
  transfers between devices with their start and end apart: 5, of which 4 were waited for; matrix products, arithmetic and copies ran while one was open for 0% of the time, Pallas kernels for 0%

profile of v2, /device:TPU:1, one launch (start us, length us, event | category | flops | bytes accessed | tf_op | source)
XLA Modules:
  0.0 101.9 jit_solution(6004308755048049804)
XLA Ops:
  0.0 0.0 copy-start.2
  0.0 0.7 copy-done.2
  0.7 1.7 %pack_line.1 = bf16[16,88,128]{2,1,0:T(8,128)(2,1)S(1)} custom-call(s32[8]{0:T(128)S(1)} %copy-done.2, bf16[3,2304]{1,0:T(4,128)(2,1)} %refs_0_.2, f32[12,1,64]{2,1,0:T(1,128)} %bitcast.14, bf16[120,256]{1,0:T(8,128)(2,1)} %bitcast.11, bf16[24,768]{1,0:T(8,128)(2,1)} %refs_3_.1), custom_call_target="tpu_custom_call" | custom-call | tf_op jit(solution)/shard_map/pack_line/pallas_call | solution.py:368
  2.3 34.9 %all_to_all.15.got_ref = bf16[16,88,128]{2,1,0:T(8,128)(2,1)S(1)} all-to-all(bf16[16,88,128]{2,1,0:T(8,128)(2,1)S(1)} %pack_line.1), channel_id=1, replica_groups=mesh['s'=8,'x'=4,'w'=2,'y'=4,'c'=2] {'s','w'}, dimensions={0} | all-to-all | bytes 720896 | tf_op jit(solution)/shard_map/all_to_all | solution.py:385
  37.2 1.5 %pack_plane.1 = (bf16[32,208,128]{2,1,0:T(8,128)(2,1)}, bf16[96,64]{1,0:T(8,128)(2,1)}) custom-call(bf16[16,88,128]{2,1,0:T(8,128)(2,1)S(1)} %all_to_all.15.got_ref), custom_call_target="tpu_custom_call" | custom-call | tf_op jit(solution)/shard_map/pack_plane/pallas_call | solution.py:388
  38.7 0.0 copy-start.7
  38.7 0.0 copy-start.8
  38.7 0.0 copy-start.1
  38.7 12.0 %all-to-all-start.1 = ((bf16[32,208,128]{2,1,0:T(8,128)(2,1)}), bf16[32,208,128]{2,1,0:T(8,128)(2,1)S(1)}, u32[]{:S(2)}, u32[]{:S(2)}) async-start(bf16[32,208,128]{2,1,0:T(8,128)(2,1)} %get-tuple-element.9), calls=%async_computation.1 | async-start | bytes 3407872 | tf_op jit(solution)/shard_map/all_to_all | solution.py:404
  50.8 0.0 copy-done.7
  50.8 0.0 copy-done.8
  50.8 5.4 %collective-permute-start = (f32[128,96]{1,0:T(8,128)S(1)}, f32[128,96]{1,0:T(8,128)S(1)}, u32[]{:S(2)}, u32[]{:S(2)}) collective-permute-start(f32[128,96]{1,0:T(8,128)S(1)} %pad_maximum_fusion), channel_id=1, source_target_pairs={{0,64},{64,128},{128,192},{192,256},{256,320},{320,384},{384,448},... | collective-permute-start | bytes 147464 | tf_op jit(solution)/shard_map/ppermute | solution.py:348
  56.2 6.5 %collective-permute-done.state_ref.refs_4_ = f32[128,96]{1,0:T(8,128)S(1)} collective-permute-done((f32[128,96]{1,0:T(8,128)S(1)}, f32[128,96]{1,0:T(8,128)S(1)}, u32[]{:S(2)}, u32[]{:S(2)}) %collective-permute-start) | collective-permute-done | bytes 49184 | tf_op jit(solution)/shard_map/ppermute | solution.py:348
  62.8 0.0 copy-start.6
  62.8 12.1 %all-to-all-done.1.got_ref = bf16[32,208,128]{2,1,0:T(8,128)(2,1)S(1)} async-done(((bf16[32,208,128]{2,1,0:T(8,128)(2,1)}), bf16[32,208,128]{2,1,0:T(8,128)(2,1)S(1)}, u32[]{:S(2)}, u32[]{:S(2)}) %all-to-all-start.1) | async-done | bytes 1703968 | tf_op jit(solution)/shard_map/all_to_all | solution.py:404
  74.8 0.0 copy-done.6
  74.8 0.0 copy-done.1
  74.8 2.2 %fold_block.1 = (bf16[32,80,128]{2,1,0:T(8,128)(2,1)}, f32[64,128]{1,0:T(8,128)}) custom-call(bf16[32,208,128]{2,1,0:T(8,128)(2,1)S(1)} %all-to-all-done.1.got_ref, bf16[64,1536]{1,0:T(8,128)(2,1)S(1)} %copy-done.1, f32[128,96]{1,0:T(8,128)} %copy-done.6), custom_call_target="tpu_custom_call" | custom-call | tf_op jit(solution)/shard_map/fold_block/pallas_call | solution.py:406
  77.1 4.3 %all-to-all-start.2 = ((bf16[32,80,128]{2,1,0:T(8,128)(2,1)}), bf16[32,80,128]{2,1,0:T(8,128)(2,1)S(1)}, u32[]{:S(2)}, u32[]{:S(2)}) async-start(bf16[32,80,128]{2,1,0:T(8,128)(2,1)} %get-tuple-element.10), calls=%async_computation.2 | async-start | bytes 1310720 | tf_op jit(solution)/shard_map/all_to_all | solution.py:433
  81.4 0.2 unpack_wo.1.refs_11_
  81.6 0.0 copy-start
  81.6 0.0 copy-start.3
  81.6 0.1 fusion
  81.7 2.3 %collective-permute-start.2 = (bf16[384,768]{1,0:T(8,128)(2,1)S(1)}, bf16[384,768]{1,0:T(8,128)(2,1)S(1)}, u32[]{:S(2)}, u32[]{:S(2)}) collective-permute-start(bf16[384,768]{1,0:T(8,128)(2,1)S(1)} %get-tuple-element.13), channel_id=1, source_target_pairs={{0,1},{1,0},{2,3},{3,2},{4,5},{5,4},{6,7},{7,6},{8,9},{9,8},{10,11... | collective-permute-start | bytes 1769480 | tf_op jit(solution)/shard_map/ppermute | solution.py:348
  83.9 2.1 %collective-permute-start.1 = (bf16[384,768]{1,0:T(8,128)(2,1)S(1)}, bf16[384,768]{1,0:T(8,128)(2,1)S(1)}, u32[]{:S(2)}, u32[]{:S(2)}) collective-permute-start(bf16[384,768]{1,0:T(8,128)(2,1)S(1)} %get-tuple-element.14), channel_id=1, source_target_pairs={{0,1},{1,0},{2,3},{3,2},{4,5},{5,4},{6,7},{7,6},{8,9},{9,8},{10,11... | collective-permute-start | bytes 1769480 | tf_op jit(solution)/shard_map/ppermute | solution.py:348
  87.3 0.0 collective-permute-done.2.refs_13_
  87.3 0.0 copy-start.4
  87.3 0.5 collective-permute-done.1.refs_12_
  87.8 0.0 copy-start.5
  87.8 6.6 %all-to-all-done.2.refs_3_ = bf16[32,80,128]{2,1,0:T(8,128)(2,1)S(1)} async-done(((bf16[32,80,128]{2,1,0:T(8,128)(2,1)}), bf16[32,80,128]{2,1,0:T(8,128)(2,1)S(1)}, u32[]{:S(2)}, u32[]{:S(2)}) %all-to-all-start.2) | async-done | bytes 655392 | tf_op jit(solution)/shard_map/all_to_all | solution.py:433
  94.4 0.0 copy-done
  94.4 0.0 copy-done.4
  94.4 0.0 copy-done.5
  94.4 0.0 copy-done.3
  94.4 7.5 %finish.1 = f32[64,96]{1,0:T(8,128)} custom-call(s32[1]{0:T(128)S(6)} %copy.14.refs_0_, s32[1]{0:T(128)S(6)} %copy.15.refs_1_, s32[8]{0:T(128)S(1)} %copy-done.3, bf16[32,80,128]{2,1,0:T(8,128)(2,1)S(1)} %all-to-all-done.2.refs_3_, f32[128,96]{1,0:T(8,128)} %copy-done.6, bf16[64,1536]{1,0:T(8,128)(2,1)} %refs_5_.1, ...), custom_call_target="tpu_custom_call" | custom-call | tf_op jit(solution)/shard_map/finish/pallas_call | solution.py:435
  (1 shorter events, 0.0 us)
Async XLA Ops:
  0.0 0.7 copy-start.2
  38.7 12.1 %copy-start.7 = (f32[1,1,64,96]{3,2,1,0:T(8,128)S(1)}, f32[1,1,64,96]{3,2,1,0:T(8,128)}, u32[]{:S(2)}) copy-start(f32[1,1,64,96]{3,2,1,0:T(8,128)} %param.14) | copy-start | bytes 73732
  38.7 12.1 %copy-start.8 = (f32[1,1,64,96]{3,2,1,0:T(8,128)S(1)}, f32[1,1,64,96]{3,2,1,0:T(8,128)}, u32[]{:S(2)}) copy-start(f32[1,1,64,96]{3,2,1,0:T(8,128)} %param.13) | copy-start | bytes 73732
  38.7 36.1 %copy-start.1 = (bf16[64,1536]{1,0:T(8,128)(2,1)S(1)}, bf16[64,1536]{1,0:T(8,128)(2,1)}, u32[]{:S(2)}) copy-start(bf16[64,1536]{1,0:T(8,128)(2,1)} %refs_5_.1) | copy-start | bytes 589828
  38.7 36.1 %all-to-all-start.1 = ((bf16[32,208,128]{2,1,0:T(8,128)(2,1)}), bf16[32,208,128]{2,1,0:T(8,128)(2,1)S(1)}, u32[]{:S(2)}, u32[]{:S(2)}) async-start(bf16[32,208,128]{2,1,0:T(8,128)(2,1)} %get-tuple-element.9), calls=%async_computation.1 | async-start | bytes 3407872 | tf_op jit(solution)/shard_map/all_to_all | solution.py:404
  50.8 12.0 %collective-permute-start = (f32[128,96]{1,0:T(8,128)S(1)}, f32[128,96]{1,0:T(8,128)S(1)}, u32[]{:S(2)}, u32[]{:S(2)}) collective-permute-start(f32[128,96]{1,0:T(8,128)S(1)} %pad_maximum_fusion), channel_id=1, source_target_pairs={{0,64},{64,128},{128,192},{192,256},{256,320},{320,384},{384,448},... | collective-permute-start | bytes 147464 | tf_op jit(solution)/shard_map/ppermute | solution.py:348
  62.8 12.1 %copy-start.6 = (f32[128,96]{1,0:T(8,128)}, f32[128,96]{1,0:T(8,128)S(1)}, u32[]{:S(2)}) copy-start(f32[128,96]{1,0:T(8,128)S(1)} %collective-permute-done.state_ref.refs_4_) | copy-start | bytes 147460
  77.1 17.3 %all-to-all-start.2 = ((bf16[32,80,128]{2,1,0:T(8,128)(2,1)}), bf16[32,80,128]{2,1,0:T(8,128)(2,1)S(1)}, u32[]{:S(2)}, u32[]{:S(2)}) async-start(bf16[32,80,128]{2,1,0:T(8,128)(2,1)} %get-tuple-element.10), calls=%async_computation.2 | async-start | bytes 1310720 | tf_op jit(solution)/shard_map/all_to_all | solution.py:433
  81.6 12.8 %copy-start = (bf16[768,768]{1,0:T(8,128)(2,1)}, bf16[768,768]{1,0:T(8,128)(2,1)S(1)}, u32[]{:S(2)}) copy-start(bf16[768,768]{1,0:T(8,128)(2,1)S(1)} %unpack_wo.1.refs_11_) | copy-start | bytes 3538948
  81.6 12.8 %copy-start.3 = (s32[8]{0:T(128)S(1)}, s32[8]{0:T(128)}, u32[]{:S(2)}) copy-start(s32[8]{0:T(128)} %refs_2_.1) | copy-start | bytes 100
  81.7 5.6 %collective-permute-start.2 = (bf16[384,768]{1,0:T(8,128)(2,1)S(1)}, bf16[384,768]{1,0:T(8,128)(2,1)S(1)}, u32[]{:S(2)}, u32[]{:S(2)}) collective-permute-start(bf16[384,768]{1,0:T(8,128)(2,1)S(1)} %get-tuple-element.13), channel_id=1, source_target_pairs={{0,1},{1,0},{2,3},{3,2},{4,5},{5,4},{6,7},{7,6},{8,9},{9,8},{10,11... | collective-permute-start | bytes 1769480 | tf_op jit(solution)/shard_map/ppermute | solution.py:348
  83.9 3.9 %collective-permute-start.1 = (bf16[384,768]{1,0:T(8,128)(2,1)S(1)}, bf16[384,768]{1,0:T(8,128)(2,1)S(1)}, u32[]{:S(2)}, u32[]{:S(2)}) collective-permute-start(bf16[384,768]{1,0:T(8,128)(2,1)S(1)} %get-tuple-element.14), channel_id=1, source_target_pairs={{0,1},{1,0},{2,3},{3,2},{4,5},{5,4},{6,7},{7,6},{8,9},{9,8},{10,11... | collective-permute-start | bytes 1769480 | tf_op jit(solution)/shard_map/ppermute | solution.py:348
  87.3 7.1 %copy-start.4 = (bf16[384,768]{1,0:T(8,128)(2,1)}, bf16[384,768]{1,0:T(8,128)(2,1)S(1)}, u32[]{:S(2)}) copy-start(bf16[384,768]{1,0:T(8,128)(2,1)S(1)} %collective-permute-done.2.refs_13_) | copy-start | bytes 1769476
  87.8 6.6 %copy-start.5 = (bf16[384,768]{1,0:T(8,128)(2,1)}, bf16[384,768]{1,0:T(8,128)(2,1)S(1)}, u32[]{:S(2)}) copy-start(bf16[384,768]{1,0:T(8,128)(2,1)S(1)} %collective-permute-done.1.refs_12_) | copy-start | bytes 1769476

commit v3 on v2

--- a/solution.py
+++ b/solution.py
@@ -17,8 +17,8 @@
 QKV_BLOCKS = 18
 KV_BLOCKS = 12
 LINE_ROWS = 88
-MSG_ROWS = 64
-PLANE_ROWS = 208
+MSG_ROWS = 56
+PLANE_ROWS = 200
 MOD_ROWS = 80
 PLANE = ("x", "y", "c")
 LINE = ("s", "w")
@@ -36,14 +36,15 @@
     return lax.dot_general(left, right, (((1,), (1,)), ((), ())), preferred_element_type=f32)
 
 
-def pack_line(times_ref, *refs):
-    out_ref, held, wo_held, w_qkv_ref, finished_ref, w_time_ref, wo_ref, arrived = refs[4:]
+def pack_line(*refs):
+    out_ref, held, wo_held, times_ref, w_qkv_ref, finished_ref, w_time_ref, wo_ref, arrived = refs[5:]
     copies = [
         pltpu.make_async_copy(source, target, arrived.at[place])
-        for place, (source, target) in enumerate(zip(refs[:4], refs[7:11]))
+        for place, (source, target) in enumerate(zip(refs[:5], refs[8:13]))
     ]
     for copy in copies:
         copy.start()
+    copies[0].wait()
     place = lax.broadcasted_iota(jnp.int32, (16, LANES), 0)
     times = jnp.zeros((16, LANES), f32)
     for step in range(STEPS):
@@ -51,7 +52,7 @@
     lane = lax.broadcasted_iota(jnp.int32, (16, LANES), 1).astype(f32)
     phase = times * jnp.exp(-math.log(10000.0) * lane / LANES)
     embed = jnp.concatenate([jnp.cos(phase), jnp.sin(phase)], axis=1)
-    for copy in copies:
+    for copy in copies[1:]:
         copy.wait()
     rows = w_qkv_ref[...].astype(f32)
     for block in range(QKV_BLOCKS):
@@ -103,7 +104,7 @@
                 out_ref[30, 16 * row : 16 * row + 16, :] = piece
                 out_ref[31, 16 * row : 16 * row + 16, :] = piece
     mods = jnp.concatenate(
-        [wide[60:64, :], wide[LINE_ROWS + 60 : LINE_ROWS + 64, :], jnp.zeros((8, LANES), f32)], axis=0
+        [wide[60:64, :], wide[LINE_ROWS + 60 : LINE_ROWS + 64, :]], axis=0
     ).astype(bf16)
     for half in range(2):
         for block in range(HEADS):
@@ -113,8 +114,8 @@
                 ]
     halves = [wo[144 * half : 144 * (half + 1), :].astype(bf16) for half in range(2)]
     for target in range(32):
-        out_ref[target, 48:64, :] = mods
-        out_ref[target, 64:208, :] = halves[target % 2]
+        out_ref[target, 48:56, :] = mods
+        out_ref[target, 56:200, :] = halves[target % 2]
     for section in range(STEPS):
         piece = wide[pl.ds(section * 2 * LINE_ROWS + side * LINE_ROWS + 54, 6), :]
         tokens[6 * section : 6 * section + 6, :] = piece[:, 0:64]
@@ -189,8 +190,8 @@
 
 def unpack_wo(got_ref, mods_ref, out_ref):
     for pair in range(16):
-        first = got_ref[2 * pair, 64:208, :].astype(f32)
-        second = got_ref[2 * pair + 1, 64:208, :].astype(f32)
+        first = got_ref[2 * pair, 56:200, :].astype(f32)
+        second = got_ref[2 * pair + 1, 56:200, :].astype(f32)
         for block in range(HEADS):
             rows = slice(24 * block, 24 * block + 24)
             out_ref[48 * pair : 48 * pair + 48, block * LANES : (block + 1) * LANES] = jnp.concatenate(
@@ -208,25 +209,28 @@
 def finish(
     start_ref,
     count_ref,
-    times_ref,
     got_ref,
     held_refs,
     wo_refs,
     out_ref,
-    normed,
+    queries,
+    keys,
+    values,
     mixture,
     after,
+    normed,
     state_ref,
     w_in_ref,
     tokens_ref,
-    keys_ref,
-    values_ref,
     mods_ref,
     w_out_ref,
+    times_ref,
     wo,
     arrived,
 ):
-    near = (state_ref, w_in_ref, tokens_ref, keys_ref, values_ref, mods_ref, w_out_ref)
+    cached = CACHE_FR * FRAME_TOK
+    near = (state_ref, w_in_ref, tokens_ref, keys.at[0:cached], values.at[0:cached])
+    near = near + (mods_ref, w_out_ref, times_ref)
     copies = [
         pltpu.make_async_copy(source, target, arrived.at[place])
         for place, (source, target) in enumerate(zip(held_refs, near))
@@ -255,47 +259,29 @@
     done = tokens_ref[...]
     _, done_root = spread_of(product(done, w_in))
 
-    def project(rows, factor, block):
-        tail = got_ref[block, 64:80, :].astype(f32)
-        return (product(rows, got_ref[block, 0:64, :]) * factor + (tail[0:1] + tail[1:2])).astype(bf16)
-
-    start = start_ref[0]
-    count = count_ref[0]
-    frame = lax.broadcasted_iota(jnp.int32, (1, CACHE_FR * FRAME_TOK), 1) // FRAME_TOK
-    frame = frame - start
-    frame = jnp.where(frame < 0, frame + CACHE_FR, frame)
-    bias = jnp.where(frame < count, 0.0, -jnp.inf)
-    factor = 1.0 / math.sqrt(HEAD)
+    def project(rows, factor, first):
+        linear = jnp.concatenate([got_ref[first + head, 0:64, :] for head in range(HEADS)], axis=1)
+        tail = jnp.concatenate([got_ref[first + head, 64:72, :] for head in range(HEADS)], axis=1).astype(f32)
+        return (product(rows, linear) * factor + (tail[0:1] + tail[1:2])).astype(bf16)
+
+    queries[...] = project(tokens, root, 0)
+    keys[cached + 96 :, :] = project(tokens, root, HEADS)
+    values[cached + 96 :, :] = project(tokens, root, 2 * HEADS)
+    keys[cached : cached + 96, :] = project(done, done_root, 3 * HEADS)
+    values[cached : cached + 96, :] = project(done, done_root, 4 * HEADS)
     for copy in copies[3:5]:
         copy.wait()
+    frame = lax.broadcasted_iota(jnp.int32, (1, cached + 192), 1) // FRAME_TOK
+    turned = frame - start_ref[0]
+    turned = jnp.where(turned < 0, turned + CACHE_FR, turned)
+    bias = jnp.where((frame >= CACHE_FR) | (turned < count_ref[0]), 0.0, -jnp.inf)
+    factor = 1.0 / (math.sqrt(HEAD) * math.log(2.0))
     for head in range(HEADS):
         columns = slice(head * HEAD, (head + 1) * HEAD)
-        query = project(tokens, root, head)
-        own_key = project(tokens, root, HEADS + head)
-        own_value = project(tokens, root, 2 * HEADS + head)
-        done_key = project(done, done_root, 3 * HEADS + head)
-        done_value = project(done, done_root, 4 * HEADS + head)
-        held = product_t(query, keys_ref[:, columns]) * factor + bias
-        own = product_t(query, own_key) * factor
-        last = product_t(query, done_key) * factor
-        highest = jnp.maximum(
-            jnp.max(held, axis=-1, keepdims=True),
-            jnp.maximum(jnp.max(own, axis=-1, keepdims=True), jnp.max(last, axis=-1, keepdims=True)),
-        )
-        held = jnp.exp(held - highest)
-        own = jnp.exp(own - highest)
-        last = jnp.exp(last - highest)
-        total = (
-            jnp.sum(held, axis=-1, keepdims=True)
-            + jnp.sum(own, axis=-1, keepdims=True)
-            + jnp.sum(last, axis=-1, keepdims=True)
-        )
-        share = 1.0 / total
-        mixture[:, columns] = (
-            product((held * share).astype(bf16), values_ref[:, columns])
-            + product((own * share).astype(bf16), own_value)
-            + product((last * share).astype(bf16), done_value)
-        ).astype(bf16)
+        scores = product_t(queries[:, columns], keys[:, columns]) + bias
+        scores = jnp.exp2((scores - jnp.max(scores, axis=-1, keepdims=True)) * factor)
+        share = 1.0 / jnp.sum(scores, axis=-1, keepdims=True)
+        mixture[:, columns] = (product(scores.astype(bf16), values[:, columns]) * share).astype(bf16)
     mixed = mixture[...]
     for copy in copies[5:]:
         copy.wait()
@@ -317,7 +303,9 @@
     for part in range(12):
         columns = slice(part * LANES, (part + 1) * LANES)
         value = (after[:, columns] - middle) * root
-        normed[:, columns] = (value * (1.0 + mods_ref[48 + part : 49 + part, :]) + mods_ref[36 + part : 37 + part, :]).astype(bf16)
+        normed[:, columns] = (
+            value * (1.0 + mods_ref[48 + part : 49 + part, :]) + mods_ref[36 + part : 37 + part, :]
+        ).astype(bf16)
     velocity = product_t(w_out_ref[...], normed[...])
     sigma_now, sigma_next = sigmas(times_ref)
     out_ref[...] = (1.0 - sigma_next) * (current - sigma_now * velocity) + sigma_next * state_ref[64:128, :]
@@ -368,20 +356,21 @@
     message = pl.pallas_call(
         pack_line,
         out_shape=pltpu.VMEM((16, LINE_ROWS, LANES), bf16),
-        in_specs=scalars(1) + anywhere(4),
+        in_specs=anywhere(5),
         out_specs=pl.BlockSpec(memory_space=pltpu.VMEM),
         scratch_shapes=[
             pltpu.VMEM((LINE_ROWS, LANES), f32),
             pltpu.VMEM((144, LANES), f32),
+            pltpu.SMEM((STEPS,), jnp.int32),
             pltpu.VMEM(w_qkv.shape, bf16),
             pltpu.VMEM((12, 1, 64), f32),
             pltpu.VMEM((120, 256), bf16),
             pltpu.VMEM(wo_rows.shape, bf16),
-            pltpu.SemaphoreType.DMA((4,)),
+            pltpu.SemaphoreType.DMA((5,)),
         ],
         compiler_params=params,
         name="pack_line",
-    )(timesteps, *map(in_hbm, (w_qkv, jnp.transpose(finished, (2, 0, 1)), w_time.T, wo_rows)))
+    )(*map(in_hbm, (timesteps, w_qkv, jnp.transpose(finished, (2, 0, 1)), w_time.T, wo_rows)))
     got = lax.all_to_all(message, LINE, 0, 0, tiled=True)
 
     state = shifted(jnp.concatenate([latents[0, 0], renoise[0, 0]], axis=0), "s", -1)
@@ -433,35 +422,47 @@
     got = lax.all_to_all(message, PLANE, 0, 0, tiled=True)
 
     stepped = pl.pallas_call(
-        lambda *refs: finish(*refs[:4], refs[4:11], refs[11:14], *refs[14:]),
+        lambda *refs: finish(*refs[:3], refs[3:11], refs[11:14], *refs[14:]),
         out_shape=jax.ShapeDtypeStruct((64, 96), f32),
-        in_specs=scalars(3) + whole(1) + anywhere(10),
+        in_specs=scalars(2) + whole(1) + anywhere(8) + [pl.BlockSpec(memory_space=pl.ANY)] * 3,
         out_specs=pl.BlockSpec(memory_space=pltpu.VMEM),
         scratch_shapes=[
-            pltpu.VMEM((96, 1536), bf16),
+            pltpu.VMEM((96, 768), bf16),
+            pltpu.VMEM((384, 768), bf16),
+            pltpu.VMEM((384, 768), bf16),
             pltpu.VMEM((96, 768), bf16),
             pltpu.VMEM((96, 1536), f32),
+            pltpu.VMEM((96, 1536), bf16),
             pltpu.VMEM((128, 96), f32),
             pltpu.VMEM((64, 1536), bf16),
             pltpu.VMEM((96, 64), bf16),
-            pltpu.VMEM((192, 768), bf16),
-            pltpu.VMEM((192, 768), bf16),
             pltpu.VMEM((64, LANES), f32),
             pltpu.VMEM((64, 1536), bf16),
+            pltpu.SMEM((STEPS,), jnp.int32),
             pltpu.VMEM((1536, 768), bf16),
-            pltpu.SemaphoreType.DMA((15,)),
+            pltpu.SemaphoreType.DMA((16,)),
         ],
         compiler_params=params,
         name="finish",
     )(
         window_start,
         window_count,
-        timesteps,
         in_vmem(got),
         *map(
             in_hbm,
-            (state, w_in, tokens, cache_keys[0], cache_values[0], mods, w_out.T, wo_half, *wo_other),
+            (
+                state,
+                w_in,
+                tokens,
+                cache_keys[0],
+                cache_values[0],
+                mods,
+                w_out.T,
+                timesteps,
+            ),
         ),
+        wo_half,
+        *wo_other,
     )
     return stepped[None, None]
 

time: 103 us -> 99.4 us (0.965)
  Pallas kernels: 13.1 us -> 10.4 us
    pallas_call x1, Pallas kernels: 7.49 us -> 5.52 us  [per_device(): pl.pallas_call(lambda *refs: finish(*refs[:3], refs[3:11], refs[11:14], *...]
where the time goes in v3:
time: 99.4 us; the launch traced here: 97.9 us
  blocking collectives  34.9 us (35%)
  starting transfers between devices  26 us (26%)
  waiting for transfers between devices  25 us (25%)
  Pallas kernels  10.4 us (10%)
  between operations  1.4 us (1%)
    all_to_all x1, blocking collectives, per_device(): got = lax.all_to_all(message, LINE, 0, 0, tiled=True)  34.9 us
    all_to_all x2, waiting for transfers between devices, per_device(): got = lax.all_to_all(message, PLANE, 0, 0, tiled=True)  18 us
    all_to_all x2, starting transfers between devices, per_device(): got = lax.all_to_all(message, PLANE, 0, 0, tiled=True)  16.3 us
    ppermute x3, starting transfers between devices, shifted(): lax.ppermute(array, axis, [(i, (i - by) % size) for i in range(size)])  9.74 us
    ppermute x3, waiting for transfers between devices, shifted(): lax.ppermute(array, axis, [(i, (i - by) % size) for i in range(size)])  7.06 us
    pallas_call x1, Pallas kernels, per_device(): pl.pallas_call(lambda *refs: finish(*refs[:3], refs[3:11], refs[11:14], *...  5.52 us
    pallas_call x1, Pallas kernels, per_device(): pl.pallas_call(fold_block, out_shape=[pltpu.VMEM((32, MOD_ROWS, LANES), b...  2.09 us
  transfers between devices with their start and end apart: 5, of which 4 were waited for; matrix products, arithmetic and copies ran while one was open for 0% of the time, Pallas kernels for 0%

profile of v3, /device:TPU:1, one launch (start us, length us, event | category | flops | bytes accessed | tf_op | source)
XLA Modules:
  0.0 97.9 jit_solution(15758508262126930408)
XLA Ops:
  0.0 1.1 %pack_line.1 = bf16[16,88,128]{2,1,0:T(8,128)(2,1)S(1)} custom-call(s32[8]{0:T(128)} %refs_10_.1, bf16[3,2304]{1,0:T(4,128)(2,1)} %refs_1_.2, f32[12,1,64]{2,1,0:T(1,128)} %bitcast.14, bf16[120,256]{1,0:T(8,128)(2,1)} %bitcast.11, bf16[24,768]{1,0:T(8,128)(2,1)} %refs_4_.2), custom_call_target="tpu_custom_call" | custom-call | tf_op jit(solution)/shard_map/pack_line/pallas_call | solution.py:356
  1.2 34.9 %all_to_all.15.got_ref = bf16[16,88,128]{2,1,0:T(8,128)(2,1)S(1)} all-to-all(bf16[16,88,128]{2,1,0:T(8,128)(2,1)S(1)} %pack_line.1), channel_id=1, replica_groups=mesh['s'=8,'x'=4,'w'=2,'y'=4,'c'=2] {'s','w'}, dimensions={0} | all-to-all | bytes 720896 | tf_op jit(solution)/shard_map/all_to_all | solution.py:374
  36.0 1.5 %pack_plane.1 = (bf16[32,200,128]{2,1,0:T(8,128)(2,1)}, bf16[96,64]{1,0:T(8,128)(2,1)}) custom-call(bf16[16,88,128]{2,1,0:T(8,128)(2,1)S(1)} %all_to_all.15.got_ref), custom_call_target="tpu_custom_call" | custom-call | tf_op jit(solution)/shard_map/pack_plane/pallas_call | solution.py:377
  37.5 0.0 copy-start.2
  37.5 0.0 copy-start.3
  37.5 0.0 copy-start
  37.5 12.0 %all-to-all-start.1 = ((bf16[32,200,128]{2,1,0:T(8,128)(2,1)}), bf16[32,200,128]{2,1,0:T(8,128)(2,1)S(1)}, u32[]{:S(2)}, u32[]{:S(2)}) async-start(bf16[32,200,128]{2,1,0:T(8,128)(2,1)} %get-tuple-element.9), calls=%async_computation.1 | async-start | bytes 3276800 | tf_op jit(solution)/shard_map/all_to_all | solution.py:393
  49.6 0.0 copy-done.2
  49.6 0.0 copy-done.3
  49.6 5.4 %collective-permute-start = (f32[128,96]{1,0:T(8,128)S(1)}, f32[128,96]{1,0:T(8,128)S(1)}, u32[]{:S(2)}, u32[]{:S(2)}) collective-permute-start(f32[128,96]{1,0:T(8,128)S(1)} %pad_maximum_fusion), channel_id=1, source_target_pairs={{0,64},{64,128},{128,192},{192,256},{256,320},{320,384},{384,448},... | collective-permute-start | bytes 147464 | tf_op jit(solution)/shard_map/ppermute | solution.py:336
  55.0 6.5 %collective-permute-done.state_ref.refs_3_ = f32[128,96]{1,0:T(8,128)S(1)} collective-permute-done((f32[128,96]{1,0:T(8,128)S(1)}, f32[128,96]{1,0:T(8,128)S(1)}, u32[]{:S(2)}, u32[]{:S(2)}) %collective-permute-start) | collective-permute-done | bytes 49184 | tf_op jit(solution)/shard_map/ppermute | solution.py:336
  61.6 0.0 copy-start.1
  61.6 11.4 %all-to-all-done.1.got_ref = bf16[32,200,128]{2,1,0:T(8,128)(2,1)S(1)} async-done(((bf16[32,200,128]{2,1,0:T(8,128)(2,1)}), bf16[32,200,128]{2,1,0:T(8,128)(2,1)S(1)}, u32[]{:S(2)}, u32[]{:S(2)}) %all-to-all-start.1) | async-done | bytes 1638432 | tf_op jit(solution)/shard_map/all_to_all | solution.py:393
  72.9 0.0 copy-done.1
  72.9 0.0 copy-done
  73.0 2.1 %fold_block.1 = (bf16[32,80,128]{2,1,0:T(8,128)(2,1)}, f32[64,128]{1,0:T(8,128)}) custom-call(bf16[32,200,128]{2,1,0:T(8,128)(2,1)S(1)} %all-to-all-done.1.got_ref, bf16[64,1536]{1,0:T(8,128)(2,1)S(1)} %copy-done, f32[128,96]{1,0:T(8,128)} %copy-done.1), custom_call_target="tpu_custom_call" | custom-call | tf_op jit(solution)/shard_map/fold_block/pallas_call | solution.py:395
  75.0 4.3 %all-to-all-start.2 = ((bf16[32,80,128]{2,1,0:T(8,128)(2,1)}), bf16[32,80,128]{2,1,0:T(8,128)(2,1)S(1)}, u32[]{:S(2)}, u32[]{:S(2)}) async-start(bf16[32,80,128]{2,1,0:T(8,128)(2,1)} %get-tuple-element.10), calls=%async_computation.2 | async-start | bytes 1310720 | tf_op jit(solution)/shard_map/all_to_all | solution.py:422
  79.3 0.2 unpack_wo.1.refs_11_
  79.5 0.1 fusion
  79.6 2.3 %collective-permute-start.2 = (bf16[384,768]{1,0:T(8,128)(2,1)S(1)}, bf16[384,768]{1,0:T(8,128)(2,1)S(1)}, u32[]{:S(2)}, u32[]{:S(2)}) collective-permute-start(bf16[384,768]{1,0:T(8,128)(2,1)S(1)} %get-tuple-element.13), channel_id=1, source_target_pairs={{0,1},{1,0},{2,3},{3,2},{4,5},{5,4},{6,7},{7,6},{8,9},{9,8},{10,11... | collective-permute-start | bytes 1769480 | tf_op jit(solution)/shard_map/ppermute | solution.py:336
  81.9 2.1 %collective-permute-start.1 = (bf16[384,768]{1,0:T(8,128)(2,1)S(1)}, bf16[384,768]{1,0:T(8,128)(2,1)S(1)}, u32[]{:S(2)}, u32[]{:S(2)}) collective-permute-start(bf16[384,768]{1,0:T(8,128)(2,1)S(1)} %get-tuple-element.14), channel_id=1, source_target_pairs={{0,1},{1,0},{2,3},{3,2},{4,5},{5,4},{6,7},{7,6},{8,9},{9,8},{10,11... | collective-permute-start | bytes 1769480 | tf_op jit(solution)/shard_map/ppermute | solution.py:336
  85.2 0.0 collective-permute-done.2.refs_13_
  85.3 0.5 collective-permute-done.1.refs_12_
  85.8 6.6 %all-to-all-done.2.refs_2_ = bf16[32,80,128]{2,1,0:T(8,128)(2,1)S(1)} async-done(((bf16[32,80,128]{2,1,0:T(8,128)(2,1)}), bf16[32,80,128]{2,1,0:T(8,128)(2,1)S(1)}, u32[]{:S(2)}, u32[]{:S(2)}) %all-to-all-start.2) | async-done | bytes 655392 | tf_op jit(solution)/shard_map/all_to_all | solution.py:422
  92.4 5.5 %finish.1 = f32[64,96]{1,0:T(8,128)} custom-call(s32[1]{0:T(128)S(6)} %copy.14.refs_0_, s32[1]{0:T(128)S(6)} %copy.15.refs_1_, bf16[32,80,128]{2,1,0:T(8,128)(2,1)S(1)} %all-to-all-done.2.refs_2_, f32[128,96]{1,0:T(8,128)} %copy-done.1, bf16[64,1536]{1,0:T(8,128)(2,1)} %refs_4_.3, bf16[96,64]{1,0:T(8,128)(2,1)} %get-tuple-element.11.refs_5_, ...), custom_call_target="tpu_custom_call" | custom-call | tf_op jit(solution)/shard_map/finish/pallas_call | solution.py:424
  (1 shorter events, 0.0 us)
Async XLA Ops:
  37.5 12.1 %copy-start.2 = (f32[1,1,64,96]{3,2,1,0:T(8,128)S(1)}, f32[1,1,64,96]{3,2,1,0:T(8,128)}, u32[]{:S(2)}) copy-start(f32[1,1,64,96]{3,2,1,0:T(8,128)} %param.14) | copy-start | bytes 73732
  37.5 12.1 %copy-start.3 = (f32[1,1,64,96]{3,2,1,0:T(8,128)S(1)}, f32[1,1,64,96]{3,2,1,0:T(8,128)}, u32[]{:S(2)}) copy-start(f32[1,1,64,96]{3,2,1,0:T(8,128)} %param.13) | copy-start | bytes 73732
  37.5 35.4 %copy-start = (bf16[64,1536]{1,0:T(8,128)(2,1)S(1)}, bf16[64,1536]{1,0:T(8,128)(2,1)}, u32[]{:S(2)}) copy-start(bf16[64,1536]{1,0:T(8,128)(2,1)} %refs_4_.3) | copy-start | bytes 589828
  37.5 35.4 %all-to-all-start.1 = ((bf16[32,200,128]{2,1,0:T(8,128)(2,1)}), bf16[32,200,128]{2,1,0:T(8,128)(2,1)S(1)}, u32[]{:S(2)}, u32[]{:S(2)}) async-start(bf16[32,200,128]{2,1,0:T(8,128)(2,1)} %get-tuple-element.9), calls=%async_computation.1 | async-start | bytes 3276800 | tf_op jit(solution)/shard_map/all_to_all | solution.py:393
  49.6 12.0 %collective-permute-start = (f32[128,96]{1,0:T(8,128)S(1)}, f32[128,96]{1,0:T(8,128)S(1)}, u32[]{:S(2)}, u32[]{:S(2)}) collective-permute-start(f32[128,96]{1,0:T(8,128)S(1)} %pad_maximum_fusion), channel_id=1, source_target_pairs={{0,64},{64,128},{128,192},{192,256},{256,320},{320,384},{384,448},... | collective-permute-start | bytes 147464 | tf_op jit(solution)/shard_map/ppermute | solution.py:336
  61.6 11.4 %copy-start.1 = (f32[128,96]{1,0:T(8,128)}, f32[128,96]{1,0:T(8,128)S(1)}, u32[]{:S(2)}) copy-start(f32[128,96]{1,0:T(8,128)S(1)} %collective-permute-done.state_ref.refs_3_) | copy-start | bytes 147460
  75.0 17.3 %all-to-all-start.2 = ((bf16[32,80,128]{2,1,0:T(8,128)(2,1)}), bf16[32,80,128]{2,1,0:T(8,128)(2,1)S(1)}, u32[]{:S(2)}, u32[]{:S(2)}) async-start(bf16[32,80,128]{2,1,0:T(8,128)(2,1)} %get-tuple-element.10), calls=%async_computation.2 | async-start | bytes 1310720 | tf_op jit(solution)/shard_map/all_to_all | solution.py:422
  79.6 5.6 %collective-permute-start.2 = (bf16[384,768]{1,0:T(8,128)(2,1)S(1)}, bf16[384,768]{1,0:T(8,128)(2,1)S(1)}, u32[]{:S(2)}, u32[]{:S(2)}) collective-permute-start(bf16[384,768]{1,0:T(8,128)(2,1)S(1)} %get-tuple-element.13), channel_id=1, source_target_pairs={{0,1},{1,0},{2,3},{3,2},{4,5},{5,4},{6,7},{7,6},{8,9},{9,8},{10,11... | collective-permute-start | bytes 1769480 | tf_op jit(solution)/shard_map/ppermute | solution.py:336
  81.9 3.9 %collective-permute-start.1 = (bf16[384,768]{1,0:T(8,128)(2,1)S(1)}, bf16[384,768]{1,0:T(8,128)(2,1)S(1)}, u32[]{:S(2)}, u32[]{:S(2)}) collective-permute-start(bf16[384,768]{1,0:T(8,128)(2,1)S(1)} %get-tuple-element.14), channel_id=1, source_target_pairs={{0,1},{1,0},{2,3},{3,2},{4,5},{5,4},{6,7},{7,6},{8,9},{9,8},{10,11... | collective-permute-start | bytes 1769480 | tf_op jit(solution)/shard_map/ppermute | solution.py:336

commit v4 on v3

--- a/solution.py
+++ b/solution.py
@@ -16,9 +16,9 @@
 LANES = 128
 QKV_BLOCKS = 18
 KV_BLOCKS = 12
-LINE_ROWS = 88
+LINE_ROWS = 72
 MSG_ROWS = 56
-PLANE_ROWS = 200
+PLANE_ROWS = 128
 MOD_ROWS = 80
 PLANE = ("x", "y", "c")
 LINE = ("s", "w")
@@ -58,8 +58,8 @@
     for block in range(QKV_BLOCKS):
         held[3 * block : 3 * block + 3, :] = rows[:, block * LANES : (block + 1) * LANES]
     tokens = finished_ref[...].reshape(12, 64).astype(bf16).astype(f32)
-    held[54:60, 0:64] = tokens[0:6]
-    held[54:60, 64:128] = tokens[6:12]
+    tokens = jnp.concatenate([tokens[0:6], tokens[6:12]], axis=1)
+    tokens = jnp.concatenate([tokens, jnp.zeros((3, LANES), f32)], axis=0)
     w_time = w_time_ref[...]
     first = embed.astype(bf16)
     rest = embed - first.astype(f32)
@@ -68,29 +68,31 @@
     mods = product_t(first, w_time) + (product_t(second, w_time) + product_t(third, w_time))
     coarse = mods.astype(bf16).astype(f32)
     fine = mods - coarse
-    held[60:64, :] = jnp.zeros((4, LANES), f32)
-    held[62:63, 0:120] = coarse[STEPS : STEPS + 1]
-    held[63:64, 0:120] = fine[STEPS : STEPS + 1]
+    held[54:72, :] = jnp.zeros((18, LANES), f32)
+    held[56:57, 0:120] = coarse[STEPS : STEPS + 1]
+    held[57:58, 0:120] = fine[STEPS : STEPS + 1]
     wo = wo_ref[...].astype(f32)
-    section = lax.axis_index("s")
+    own_section, own_side = lax.axis_index("s"), lax.axis_index("w")
+    share = []
     for block in range(HEADS):
         wo_held[24 * block : 24 * block + 24, :] = wo[:, block * LANES : (block + 1) * LANES]
-        held[64 + 3 * block : 67 + 3 * block, :] = wo_held[pl.ds(24 * block + 3 * section, 3), :]
-    held[82:88, :] = jnp.zeros((6, LANES), f32)
+        share.append(wo_held[pl.ds(24 * block + 3 * own_section, 3), :])
+    share = [jnp.concatenate(share[0:3], axis=0), jnp.concatenate(share[3:6], axis=0)]
     common = held[0:48, :].astype(bf16)
-    wo_rows = held[64:88, :].astype(bf16)
     for section in range(STEPS):
         step = (section - 1) % STEPS
-        held[60:61, 0:120] = coarse[step : step + 1]
-        held[61:62, 0:120] = fine[step : step + 1]
-        last = held[48:64, :].astype(bf16)
+        held[54:55, 0:120] = coarse[step : step + 1]
+        held[55:56, 0:120] = fine[step : step + 1]
         for side in range(2):
+            held[58:67, :] = jnp.where(own_side == side, tokens, share[section % 2])
             out_ref[2 * section + side, 0:48, :] = common
-            out_ref[2 * section + side, 48:64, :] = last
-            out_ref[2 * section + side, 64:88, :] = wo_rows
-
-
-def pack_plane(got_ref, out_ref, finished_ref, wide, tokens, wo):
+            out_ref[2 * section + side, 48:72, :] = held[48:72, :].astype(bf16)
+
+
+def pack_plane(got_ref, wo_ref, out_ref, finished_ref, wide, tokens, far, near, arrived):
+    columns = pl.ds(pl.multiple_of(384 * lax.rem(lax.axis_index("s"), 2), LANES), 384)
+    copy = pltpu.make_async_copy(wo_ref.at[:, columns], near, arrived)
+    copy.start()
     side = lax.axis_index("w")
     for peer in range(16):
         wide[peer * LINE_ROWS : (peer + 1) * LINE_ROWS, :] = got_ref[peer].astype(f32)
@@ -104,20 +106,22 @@
                 out_ref[30, 16 * row : 16 * row + 16, :] = piece
                 out_ref[31, 16 * row : 16 * row + 16, :] = piece
     mods = jnp.concatenate(
-        [wide[60:64, :], wide[LINE_ROWS + 60 : LINE_ROWS + 64, :]], axis=0
+        [wide[54:58, :], wide[LINE_ROWS + 54 : LINE_ROWS + 58, :]], axis=0
     ).astype(bf16)
-    for half in range(2):
-        for block in range(HEADS):
-            for row in range(3):
-                wo[pl.ds(144 * half + 24 * block + row, 8, stride=3), :] = wide[
-                    pl.ds(half * LINE_ROWS + 64 + 3 * block + row, 8, stride=2 * LINE_ROWS), :
-                ]
-    halves = [wo[144 * half : 144 * (half + 1), :].astype(bf16) for half in range(2)]
+    for block in range(3):
+        for row in range(3):
+            begin = (1 - side) * LINE_ROWS + 58 + 3 * block + row
+            far[pl.ds(24 * block + row, 8, stride=3), :] = wide[pl.ds(begin, 8, stride=2 * LINE_ROWS), :]
+    copy.wait()
+    here = near[...].astype(f32)
+    here = jnp.concatenate([here[:, block * LANES : (block + 1) * LANES] for block in range(3)], axis=0)
+    there = far[...]
+    halves = [jnp.where(side == half, here, there).astype(bf16) for half in range(2)]
     for target in range(32):
         out_ref[target, 48:56, :] = mods
-        out_ref[target, 56:200, :] = halves[target % 2]
+        out_ref[target, 56:128, :] = halves[target % 2]
     for section in range(STEPS):
-        piece = wide[pl.ds(section * 2 * LINE_ROWS + side * LINE_ROWS + 54, 6), :]
+        piece = wide[pl.ds(section * 2 * LINE_ROWS + side * LINE_ROWS + 58, 6), :]
         tokens[6 * section : 6 * section + 6, :] = piece[:, 0:64]
         tokens[48 + 6 * section : 54 + 6 * section, :] = piece[:, 64:128]
     finished_ref[...] = tokens[...].astype(bf16)
@@ -190,9 +194,9 @@
 
 def unpack_wo(got_ref, mods_ref, out_ref):
     for pair in range(16):
-        first = got_ref[2 * pair, 56:200, :].astype(f32)
-        second = got_ref[2 * pair + 1, 56:200, :].astype(f32)
-        for block in range(HEADS):
+        first = got_ref[2 * pair, 56:128, :].astype(f32)
+        second = got_ref[2 * pair + 1, 56:128, :].astype(f32)
+        for block in range(3):
             rows = slice(24 * block, 24 * block + 24)
             out_ref[48 * pair : 48 * pair + 48, block * LANES : (block + 1) * LANES] = jnp.concatenate(
                 [first[rows], second[rows]], axis=0
@@ -210,6 +214,8 @@
     start_ref,
     count_ref,
     got_ref,
+    state_ref,
+    w_in_ref,
     held_refs,
     wo_refs,
     out_ref,
@@ -219,8 +225,6 @@
     mixture,
     after,
     normed,
-    state_ref,
-    w_in_ref,
     tokens_ref,
     mods_ref,
     w_out_ref,
@@ -229,33 +233,29 @@
     arrived,
 ):
     cached = CACHE_FR * FRAME_TOK
-    near = (state_ref, w_in_ref, tokens_ref, keys.at[0:cached], values.at[0:cached])
-    near = near + (mods_ref, w_out_ref, times_ref)
+    near = (tokens_ref, keys.at[0:cached], values.at[0:cached], mods_ref, w_out_ref, times_ref)
     copies = [
         pltpu.make_async_copy(source, target, arrived.at[place])
         for place, (source, target) in enumerate(zip(held_refs, near))
     ]
-    core = lax.axis_index("c")
-    for half, side in enumerate((core, 1 - core)):
+    core, odd = lax.axis_index("c"), lax.rem(lax.axis_index("s"), 2)
+    for source, side, half in zip(wo_refs, (core, core, 1 - core, 1 - core), (odd, 1 - odd) * 2):
+        columns = pl.ds(pl.multiple_of(384 * half, LANES), 384)
         for x in range(4):
-            begin = pl.multiple_of(384 * x + 192 * side, 192)
-            source, place = (wo_refs[0], x) if half == 0 else (wo_refs[1 + x // 2], x % 2)
+            rows = pl.ds(pl.multiple_of(384 * x + 192 * side, 192), 192)
             copies.append(
                 pltpu.make_async_copy(
-                    source.at[192 * place : 192 * (place + 1)],
-                    wo.at[pl.ds(begin, 192)],
-                    arrived.at[len(copies)],
+                    source.at[192 * x : 192 * (x + 1)], wo.at[rows, columns], arrived.at[len(copies)]
                 )
             )
     for copy in copies:
         copy.start()
-    for copy in copies[:3]:
-        copy.wait()
     current = state_ref[0:64, :]
     w_in = w_in_ref[...]
     tokens = current.T.astype(bf16)
     hidden = product(tokens, w_in)
     _, root = spread_of(hidden)
+    copies[0].wait()
     done = tokens_ref[...]
     _, done_root = spread_of(product(done, w_in))
 
@@ -269,7 +269,7 @@
     values[cached + 96 :, :] = project(tokens, root, 2 * HEADS)
     keys[cached : cached + 96, :] = project(done, done_root, 3 * HEADS)
     values[cached : cached + 96, :] = project(done, done_root, 4 * HEADS)
-    for copy in copies[3:5]:
+    for copy in copies[1:3]:
         copy.wait()
     frame = lax.broadcasted_iota(jnp.int32, (1, cached + 192), 1) // FRAME_TOK
     turned = frame - start_ref[0]
@@ -283,7 +283,7 @@
         share = 1.0 / jnp.sum(scores, axis=-1, keepdims=True)
         mixture[:, columns] = (product(scores.astype(bf16), values[:, columns]) * share).astype(bf16)
     mixed = mixture[...]
-    for copy in copies[5:]:
+    for copy in copies[3:]:
         copy.wait()
     sums = jnp.zeros((tokens.shape[0], LANES), f32)
     for part in range(12):
@@ -336,6 +336,17 @@
     return lax.ppermute(array, axis, [(i, (i - by) % size) for i in range(size)])
 
 
+def neighbour_planes():
+    def place(chip, core):
+        return (chip % 8 * 2 + chip // 8) * 2 + core
+
+    return [
+        (place(chip, core), place((chip + 1 if (chip + core) % 2 == 0 else chip - 1) % 16, core))
+        for chip in range(16)
+        for core in range(2)
+    ]
+
+
 def per_device(
     latents,
     renoise,
@@ -380,16 +391,18 @@
             pltpu.VMEM((32, PLANE_ROWS, LANES), bf16),
             pltpu.HBM((96, 64), bf16),
         ],
-        in_specs=whole(1),
+        in_specs=whole(1) + anywhere(1),
         out_specs=whole(2),
         scratch_shapes=[
             pltpu.VMEM((16 * LINE_ROWS, LANES), f32),
             pltpu.VMEM((96, 64), f32),
-            pltpu.VMEM((288, LANES), f32),
+            pltpu.VMEM((72, LANES), f32),
+            pltpu.VMEM((24, 384), bf16),
+            pltpu.SemaphoreType.DMA(()),
         ],
         compiler_params=params,
         name="pack_plane",
-    )(in_vmem(got))
+    )(in_vmem(got), in_hbm(wo_rows))
     got = lax.all_to_all(message, PLANE, 0, 0, tiled=True)
 
     message, mods = pl.pallas_call(
@@ -409,22 +422,23 @@
         ],
         compiler_params=params,
         name="fold_block",
-    )(in_vmem(got), w_in, in_hbm(state))
+    )(in_vmem(got), in_vmem(w_in), in_vmem(state))
     wo_half = pl.pallas_call(
         unpack_wo,
-        out_shape=pltpu.VMEM((768, 768), bf16),
+        out_shape=pltpu.VMEM((768, 384), bf16),
         in_specs=whole(1) + anywhere(1),
         out_specs=pl.BlockSpec(memory_space=pltpu.VMEM),
         compiler_params=params,
         name="unpack_wo",
     )(in_vmem(got), in_hbm(mods))
-    wo_other = [shifted(wo_half[384 * part : 384 * (part + 1)], "c", 1) for part in range(2)]
+    wo_next = lax.ppermute(wo_half, ("s", "w", "c"), neighbour_planes())
+    wo_all = [wo_half, wo_next, shifted(wo_half, "c", 1), shifted(wo_next, "c", 1)]
     got = lax.all_to_all(message, PLANE, 0, 0, tiled=True)
 
     stepped = pl.pallas_call(
-        lambda *refs: finish(*refs[:3], refs[3:11], refs[11:14], *refs[14:]),
+        lambda *refs: finish(*refs[:5], refs[5:11], refs[11:15], *refs[15:]),
         out_shape=jax.ShapeDtypeStruct((64, 96), f32),
-        in_specs=scalars(2) + whole(1) + anywhere(8) + [pl.BlockSpec(memory_space=pl.ANY)] * 3,
+        in_specs=scalars(2) + whole(3) + anywhere(6) + [pl.BlockSpec(memory_space=pl.ANY)] * 4,
         out_specs=pl.BlockSpec(memory_space=pltpu.VMEM),
         scratch_shapes=[
             pltpu.VMEM((96, 768), bf16),
@@ -433,36 +447,21 @@
             pltpu.VMEM((96, 768), bf16),
             pltpu.VMEM((96, 1536), f32),
             pltpu.VMEM((96, 1536), bf16),
-            pltpu.VMEM((128, 96), f32),
-            pltpu.VMEM((64, 1536), bf16),
             pltpu.VMEM((96, 64), bf16),
             pltpu.VMEM((64, LANES), f32),
             pltpu.VMEM((64, 1536), bf16),
             pltpu.SMEM((STEPS,), jnp.int32),
             pltpu.VMEM((1536, 768), bf16),
-            pltpu.SemaphoreType.DMA((16,)),
+            pltpu.SemaphoreType.DMA((22,)),
         ],
         compiler_params=params,
         name="finish",
     )(
         window_start,
         window_count,
-        in_vmem(got),
-        *map(
-            in_hbm,
-            (
-                state,
-                w_in,
-                tokens,
-                cache_keys[0],
-                cache_values[0],
-                mods,
-                w_out.T,
-                timesteps,
-            ),
-        ),
-        wo_half,
-        *wo_other,
+        *map(in_vmem, (got, state, w_in)),
+        *map(in_hbm, (tokens, cache_keys[0], cache_values[0], mods, w_out.T, timesteps)),
+        *wo_all,
     )
     return stepped[None, None]
 

time: 99.4 us -> 94.6 us (0.952)
  waiting for transfers between devices: 25 us -> 17.5 us
  starting transfers between devices: 26 us -> 33 us
  blocking collectives: 34.9 us -> 31.8 us
    all_to_all x2, waiting for transfers between devices: 18 us -> 10.6 us  [per_device(): got = lax.all_to_all(message, PLANE, 0, 0, tiled=True)]
    ppermute x0 -> x1, starting transfers between devices: none -> 3.19 us  [per_device(): wo_next = lax.ppermute(wo_half, ('s', 'w', 'c'), neighbour_planes())]
    all_to_all x1, blocking collectives: 34.9 us -> 31.8 us  [per_device(): got = lax.all_to_all(message, LINE, 0, 0, tiled=True)]
    all_to_all x2, starting transfers between devices: 16.3 us -> 18.8 us  [per_device(): got = lax.all_to_all(message, PLANE, 0, 0, tiled=True)]
    ppermute x3, starting transfers between devices: 9.74 us -> 11 us  [shifted(): lax.ppermute(array, axis, [(i, (i - by) % size) for i in range(size)])]
  transfers between devices with their start and end apart: 5 -> 6, of which waited for: 4 -> 4; matrix products, arithmetic and copies ran while one was open for 0% -> 0% of each run, Pallas kernels for 0% -> 0%
where the time goes in v4:
time: 94.6 us; the launch traced here: 94 us
  starting transfers between devices  33 us (35%)
  blocking collectives  31.8 us (34%)
  waiting for transfers between devices  17.5 us (18%)
  Pallas kernels  10.3 us (11%)
  between operations  1.42 us (2%)
    all_to_all x1, blocking collectives, per_device(): got = lax.all_to_all(message, LINE, 0, 0, tiled=True)  31.8 us
    all_to_all x2, starting transfers between devices, per_device(): got = lax.all_to_all(message, PLANE, 0, 0, tiled=True)  18.8 us
    ppermute x3, starting transfers between devices, shifted(): lax.ppermute(array, axis, [(i, (i - by) % size) for i in range(size)])  11 us
    all_to_all x2, waiting for transfers between devices, per_device(): got = lax.all_to_all(message, PLANE, 0, 0, tiled=True)  10.6 us
    ppermute x3, waiting for transfers between devices, shifted(): lax.ppermute(array, axis, [(i, (i - by) % size) for i in range(size)])  6.69 us
    pallas_call x1, Pallas kernels, per_device(): pl.pallas_call(lambda *refs: finish(*refs[:5], refs[5:11], refs[11:15], *...  5.13 us
    ppermute x1, starting transfers between devices, per_device(): wo_next = lax.ppermute(wo_half, ('s', 'w', 'c'), neighbour_planes())  3.19 us
    pallas_call x1, Pallas kernels, per_device(): pl.pallas_call(fold_block, out_shape=[pltpu.VMEM((32, MOD_ROWS, LANES), b...  2.09 us
  transfers between devices with their start and end apart: 6, of which 4 were waited for; matrix products, arithmetic and copies ran while one was open for 0% of the time, Pallas kernels for 0%

profile of v4, /device:TPU:1, one launch (start us, length us, event | category | flops | bytes accessed | tf_op | source)
XLA Modules:
  0.0 94.0 jit_solution(4732111094130978989)
XLA Ops:
  0.0 1.2 %pack_line.1 = bf16[16,72,128]{2,1,0:T(8,128)(2,1)S(1)} custom-call(s32[8]{0:T(128)} %refs_10_.1, bf16[3,2304]{1,0:T(4,128)(2,1)} %refs_1_.2, f32[12,1,64]{2,1,0:T(1,128)} %bitcast.14, bf16[120,256]{1,0:T(8,128)(2,1)} %bitcast.11, bf16[24,768]{1,0:T(8,128)(2,1)} %wo_ref.1), custom_call_target="tpu_custom_call" | custom-call | tf_op jit(solution)/shard_map/pack_line/pallas_call | solution.py:367
  1.2 31.8 %all_to_all.15.got_ref = bf16[16,72,128]{2,1,0:T(8,128)(2,1)S(1)} all-to-all(bf16[16,72,128]{2,1,0:T(8,128)(2,1)S(1)} %pack_line.1), channel_id=1, replica_groups=mesh['s'=8,'x'=4,'w'=2,'y'=4,'c'=2] {'s','w'}, dimensions={0} | all-to-all | bytes 589824 | tf_op jit(solution)/shard_map/all_to_all | solution.py:385
  33.0 1.8 %pack_plane.1 = (bf16[32,128,128]{2,1,0:T(8,128)(2,1)}, bf16[96,64]{1,0:T(8,128)(2,1)}) custom-call(bf16[16,72,128]{2,1,0:T(8,128)(2,1)S(1)} %all_to_all.15.got_ref, bf16[24,768]{1,0:T(8,128)(2,1)} %wo_ref.1), custom_call_target="tpu_custom_call" | custom-call | tf_op jit(solution)/shard_map/pack_plane/pallas_call | solution.py:388
  34.8 0.0 copy-start.1
  34.8 0.0 copy-start.2
  34.8 0.0 copy-start
  34.8 12.5 %all-to-all-start.1 = ((bf16[32,128,128]{2,1,0:T(8,128)(2,1)}), bf16[32,128,128]{2,1,0:T(8,128)(2,1)S(1)}, u32[]{:S(2)}, u32[]{:S(2)}) async-start(bf16[32,128,128]{2,1,0:T(8,128)(2,1)} %get-tuple-element.9), calls=%async_computation.1 | async-start | bytes 2097152 | tf_op jit(solution)/shard_map/all_to_all | solution.py:406
  47.3 0.0 copy-done.1
  47.3 0.0 copy-done.2
  47.4 5.3 %collective-permute-start = (f32[128,96]{1,0:T(8,128)S(1)}, f32[128,96]{1,0:T(8,128)S(1)}, u32[]{:S(2)}, u32[]{:S(2)}) collective-permute-start(f32[128,96]{1,0:T(8,128)S(1)} %pad_maximum_fusion), channel_id=1, source_target_pairs={{0,64},{64,128},{128,192},{192,256},{256,320},{320,384},{384,448},... | collective-permute-start | bytes 147464 | tf_op jit(solution)/shard_map/ppermute | solution.py:336
  52.6 6.7 %collective-permute-done.state_ref.refs_3_ = f32[128,96]{1,0:T(8,128)S(1)} collective-permute-done((f32[128,96]{1,0:T(8,128)S(1)}, f32[128,96]{1,0:T(8,128)S(1)}, u32[]{:S(2)}, u32[]{:S(2)}) %collective-permute-start) | collective-permute-done | bytes 49184 | tf_op jit(solution)/shard_map/ppermute | solution.py:336
  59.3 4.9 %all-to-all-done.1.got_ref = bf16[32,128,128]{2,1,0:T(8,128)(2,1)S(1)} async-done(((bf16[32,128,128]{2,1,0:T(8,128)(2,1)}), bf16[32,128,128]{2,1,0:T(8,128)(2,1)S(1)}, u32[]{:S(2)}, u32[]{:S(2)}) %all-to-all-start.1) | async-done | bytes 1048608 | tf_op jit(solution)/shard_map/all_to_all | solution.py:406
  64.2 0.0 copy-done
  64.2 2.1 %fold_block.1 = (bf16[32,80,128]{2,1,0:T(8,128)(2,1)}, f32[64,128]{1,0:T(8,128)}) custom-call(bf16[32,128,128]{2,1,0:T(8,128)(2,1)S(1)} %all-to-all-done.1.got_ref, bf16[64,1536]{1,0:T(8,128)(2,1)S(1)} %copy-done, f32[128,96]{1,0:T(8,128)S(1)} %collective-permute-done.state_ref.refs_3_), custom_call_target="tpu_custom_call" | custom-call | tf_op jit(solution)/shard_map/fold_block/pallas_call | solution.py:408
  66.3 0.1 unpack_wo.1.refs_11_
  66.4 3.2 %collective-permute-start.1 = (bf16[768,384]{1,0:T(8,128)(2,1)S(1)}, bf16[768,384]{1,0:T(8,128)(2,1)S(1)}, u32[]{:S(2)}, u32[]{:S(2)}) collective-permute-start(bf16[768,384]{1,0:T(8,128)(2,1)S(1)} %unpack_wo.1.refs_11_), channel_id=1, source_target_pairs={{0,64},{1,457},{64,0},{65,129},{128,192},{129,65},{192,128},{193,2... | collective-permute-start | bytes 1769480 | tf_op jit(solution)/shard_map/ppermute | solution.py:434
  69.6 6.3 %all-to-all-start.2 = ((bf16[32,80,128]{2,1,0:T(8,128)(2,1)}), bf16[32,80,128]{2,1,0:T(8,128)(2,1)S(1)}, u32[]{:S(2)}, u32[]{:S(2)}) async-start(bf16[32,80,128]{2,1,0:T(8,128)(2,1)} %get-tuple-element.10), calls=%async_computation.2 | async-start | bytes 1310720 | tf_op jit(solution)/shard_map/all_to_all | solution.py:436
  76.0 2.1 %collective-permute-start.2 = (bf16[768,384]{1,0:T(8,128)(2,1)S(1)}, bf16[768,384]{1,0:T(8,128)(2,1)S(1)}, u32[]{:S(2)}, u32[]{:S(2)}) collective-permute-start(bf16[768,384]{1,0:T(8,128)(2,1)S(1)} %unpack_wo.1.refs_11_), channel_id=1, source_target_pairs={{0,1},{1,0},{2,3},{3,2},{4,5},{5,4},{6,7},{7,6},{8,9},{9,8},{10,11... | collective-permute-start | bytes 1769480 | tf_op jit(solution)/shard_map/ppermute | solution.py:336
  78.1 0.2 collective-permute-done.1.refs_12_
  78.3 3.6 %collective-permute-start.3 = (bf16[768,384]{1,0:T(8,128)(2,1)S(1)}, bf16[768,384]{1,0:T(8,128)(2,1)}, u32[]{:S(2)}, u32[]{:S(2)}) collective-permute-start(bf16[768,384]{1,0:T(8,128)(2,1)S(1)} %collective-permute-done.1.refs_12_), channel_id=1, source_target_pairs={{0,1},{1,0},{2,3},{3,2},{4,5},{5,4},{6,7},{7,6},{8,9},{9,8},{10,11... | collective-permute-start | bytes 1769480 | tf_op jit(solution)/shard_map/ppermute | solution.py:336
  83.2 0.0 collective-permute-done.2.refs_13_
  83.2 5.7 %all-to-all-done.2.refs_2_ = bf16[32,80,128]{2,1,0:T(8,128)(2,1)S(1)} async-done(((bf16[32,80,128]{2,1,0:T(8,128)(2,1)}), bf16[32,80,128]{2,1,0:T(8,128)(2,1)S(1)}, u32[]{:S(2)}, u32[]{:S(2)}) %all-to-all-start.2) | async-done | bytes 655392 | tf_op jit(solution)/shard_map/all_to_all | solution.py:436
  88.9 0.0 collective-permute-done.3.refs_14_
  88.9 5.1 %finish.1 = f32[64,96]{1,0:T(8,128)} custom-call(s32[1]{0:T(128)S(6)} %copy.14.refs_0_, s32[1]{0:T(128)S(6)} %copy.15.refs_1_, bf16[32,80,128]{2,1,0:T(8,128)(2,1)S(1)} %all-to-all-done.2.refs_2_, f32[128,96]{1,0:T(8,128)S(1)} %collective-permute-done.state_ref.refs_3_, bf16[64,1536]{1,0:T(8,128)(2,1)S(1)} %copy-done, ...), custom_call_target="tpu_custom_call" | custom-call | tf_op jit(solution)/shard_map/finish/pallas_call | solution.py:438
  (1 shorter events, 0.0 us)
Async XLA Ops:
  34.8 12.6 %copy-start.1 = (f32[1,1,64,96]{3,2,1,0:T(8,128)S(1)}, f32[1,1,64,96]{3,2,1,0:T(8,128)}, u32[]{:S(2)}) copy-start(f32[1,1,64,96]{3,2,1,0:T(8,128)} %param.14) | copy-start | bytes 73732
  34.8 12.6 %copy-start.2 = (f32[1,1,64,96]{3,2,1,0:T(8,128)S(1)}, f32[1,1,64,96]{3,2,1,0:T(8,128)}, u32[]{:S(2)}) copy-start(f32[1,1,64,96]{3,2,1,0:T(8,128)} %param.13) | copy-start | bytes 73732
  34.8 29.4 %copy-start = (bf16[64,1536]{1,0:T(8,128)(2,1)S(1)}, bf16[64,1536]{1,0:T(8,128)(2,1)}, u32[]{:S(2)}) copy-start(bf16[64,1536]{1,0:T(8,128)(2,1)} %refs_4_.3) | copy-start | bytes 589828
  34.8 29.4 %all-to-all-start.1 = ((bf16[32,128,128]{2,1,0:T(8,128)(2,1)}), bf16[32,128,128]{2,1,0:T(8,128)(2,1)S(1)}, u32[]{:S(2)}, u32[]{:S(2)}) async-start(bf16[32,128,128]{2,1,0:T(8,128)(2,1)} %get-tuple-element.9), calls=%async_computation.1 | async-start | bytes 2097152 | tf_op jit(solution)/shard_map/all_to_all | solution.py:406
  47.4 12.0 %collective-permute-start = (f32[128,96]{1,0:T(8,128)S(1)}, f32[128,96]{1,0:T(8,128)S(1)}, u32[]{:S(2)}, u32[]{:S(2)}) collective-permute-start(f32[128,96]{1,0:T(8,128)S(1)} %pad_maximum_fusion), channel_id=1, source_target_pairs={{0,64},{64,128},{128,192},{192,256},{256,320},{320,384},{384,448},... | collective-permute-start | bytes 147464 | tf_op jit(solution)/shard_map/ppermute | solution.py:336
  66.4 11.8 %collective-permute-start.1 = (bf16[768,384]{1,0:T(8,128)(2,1)S(1)}, bf16[768,384]{1,0:T(8,128)(2,1)S(1)}, u32[]{:S(2)}, u32[]{:S(2)}) collective-permute-start(bf16[768,384]{1,0:T(8,128)(2,1)S(1)} %unpack_wo.1.refs_11_), channel_id=1, source_target_pairs={{0,64},{1,457},{64,0},{65,129},{128,192},{129,65},{192,128},{193,2... | collective-permute-start | bytes 1769480 | tf_op jit(solution)/shard_map/ppermute | solution.py:434
  69.6 19.3 %all-to-all-start.2 = ((bf16[32,80,128]{2,1,0:T(8,128)(2,1)}), bf16[32,80,128]{2,1,0:T(8,128)(2,1)S(1)}, u32[]{:S(2)}, u32[]{:S(2)}) async-start(bf16[32,80,128]{2,1,0:T(8,128)(2,1)} %get-tuple-element.10), calls=%async_computation.2 | async-start | bytes 1310720 | tf_op jit(solution)/shard_map/all_to_all | solution.py:436
  76.0 7.2 %collective-permute-start.2 = (bf16[768,384]{1,0:T(8,128)(2,1)S(1)}, bf16[768,384]{1,0:T(8,128)(2,1)S(1)}, u32[]{:S(2)}, u32[]{:S(2)}) collective-permute-start(bf16[768,384]{1,0:T(8,128)(2,1)S(1)} %unpack_wo.1.refs_11_), channel_id=1, source_target_pairs={{0,1},{1,0},{2,3},{3,2},{4,5},{5,4},{6,7},{7,6},{8,9},{9,8},{10,11... | collective-permute-start | bytes 1769480 | tf_op jit(solution)/shard_map/ppermute | solution.py:336
  78.3 10.6 %collective-permute-start.3 = (bf16[768,384]{1,0:T(8,128)(2,1)S(1)}, bf16[768,384]{1,0:T(8,128)(2,1)}, u32[]{:S(2)}, u32[]{:S(2)}) collective-permute-start(bf16[768,384]{1,0:T(8,128)(2,1)S(1)} %collective-permute-done.1.refs_12_), channel_id=1, source_target_pairs={{0,1},{1,0},{2,3},{3,2},{4,5},{5,4},{6,7},{7,6},{8,9},{9,8},{10,11... | collective-permute-start | bytes 1769480 | tf_op jit(solution)/shard_map/ppermute | solution.py:336
